TPU v7x, 32 devices: a whole 2x2x4 slice. The times are simulated.
32 devices in a mesh: by: 4 (over x, core), bx: 8 (over z, y).
Axes of the slice: x: 2, y: 2, z: 4, core: 2. Of those that a mesh axis runs over, the one named last changes fastest.
Arguments:
- tracer_one: float32 [18, 256, 2048], P(None, 'by', 'bx'), may hold values from -6 to 6
- tracer_two: float32 [18, 256, 2048], P(None, 'by', 'bx'), may hold values from -6 to 6
- east_flow: bfloat16 [18, 256, 2048], P(None, 'by', 'bx'), may hold values from -0.3984375 to 0.3984375
- north_flow: bfloat16 [18, 256, 2048], P(None, 'by', 'bx'), may hold values from -0.3984375 to 0.3984375
- depth_levels: int32 [256, 2048], P('by', 'bx'), may hold values from 0 to 18
- side_mix: float32 [18], replicated, may hold values from 0.02 to 0.2
- vert_mix: float32 [18], replicated, may hold values from 0.01 to 0.3
- thickness: float32 [18], replicated, may hold values from 0.1 to 0.4
- corner_depth: float32 [256, 2048], P('by', 'bx'), may hold values from 0.5 to 4
- diagonal: float32 [256, 2048], P('by', 'bx'), may hold values from 0.05 to 0.5
Outputs:
- new_one: float32 [18, 256, 2048], P(None, 'by', 'bx')
- new_two: float32 [18, 256, 2048], P(None, 'by', 'bx')
- surface: float32 [256, 2048], P('by', 'bx')
All inputs are finite; a program needn't handle non-finite values.
Results may differ from a plain program's by a relative error of at most 0.0003.
Values may be sent and summed in bfloat16 or wider, within the bound.
A program may use at most 192 MiB of HBM per device.

v0:
```python
import jax
import jax.numpy as jnp
from jax import lax
from jax.sharding import PartitionSpec as P

ITERS = 3


def padded_2(shard, sides, width, wrap):
    for axis, dim in sides:
        peers, length = (lax.axis_size(axis), shard.shape[dim])
        up = [(i, (i + 1) % peers) for i in range(peers if wrap else peers - 1)]
        down = [(j, i) for i, j in up]
        last = lax.slice_in_dim(shard, length - width, length, axis=dim)
        first = lax.slice_in_dim(shard, 0, width, axis=dim)
        before = lax.ppermute(last, axis, up)
        after = lax.ppermute(first, axis, down)
        shard = jnp.concatenate([before, shard, after], axis=dim)
    return shard


def horizontal(tracer_pad, east_cols, north_rows, wet_pad, side):
    left = tracer_pad[..., 1:-1, :-1]
    right = tracer_pad[..., 1:-1, 1:]
    face_east = wet_pad[..., 1:-1, :-1] * wet_pad[..., 1:-1, 1:]
    east = (east_cols * 0.5 * (left + right) - side * (right - left)) * face_east
    lower = tracer_pad[..., :-1, 1:-1]
    upper = tracer_pad[..., 1:, 1:-1]
    face_north = wet_pad[..., :-1, 1:-1] * wet_pad[..., 1:, 1:-1]
    north = (north_rows * 0.5 * (lower + upper) - side * (upper - lower)) * face_north
    return -(east[..., 1:] - east[..., :-1]) - (north[..., 1:, :] - north[..., :-1, :])


def vertical(tracers, wet, vert_mix):
    falling = vert_mix[:-1, None, None] * (tracers[:, 1:] - tracers[:, :-1]) * wet[1:]
    zeros = jnp.zeros_like(tracers[:, :1])
    padded = jnp.concatenate([zeros, falling, zeros], axis=1)
    return padded[:, 1:] - padded[:, :-1]


def corner_operator(extended, depth_ext, field, diagonal):
    cell_a = extended[:-1, :-1]
    cell_b = extended[:-1, 1:]
    cell_c = extended[1:, :-1]
    cell_d = extended[1:, 1:]
    grad_x = 0.5 * (cell_b + cell_d - (cell_a + cell_c))
    grad_y = 0.5 * (cell_c + cell_d - (cell_a + cell_b))
    flux_x = depth_ext * grad_x
    flux_y = depth_ext * grad_y
    plus = flux_x + flux_y
    minus = flux_x - flux_y
    return (
        diagonal * field
        - 0.5 * plus[1:, 1:]
        + 0.5 * minus[1:, :-1]
        - 0.5 * minus[:-1, 1:]
        + 0.5 * plus[:-1, :-1]
    )


def chron_gear(forcing, operate, totals):
    surface = jnp.zeros_like(forcing)
    residual = forcing
    image = operate(residual)
    norm_now, product = totals(residual * residual, residual * image)
    alpha = norm_now / product
    direction, along = (residual, image)
    for step in range(ITERS):
        surface = surface + alpha * direction
        residual = residual - alpha * along
        if step + 1 < ITERS:
            image = operate(residual)
            norm_next, product = totals(residual * residual, residual * image)
            ratio = norm_next / norm_now
            alpha = norm_next / (product - ratio * norm_next / alpha)
            direction = residual + ratio * direction
            along = image + ratio * along
            norm_now = norm_next
    return surface


def device_totals(first, second):
    return lax.psum((jnp.sum(first), jnp.sum(second)), ("by", "bx"))


def block_rim(field):
    widened = padded_2(field, (("bx", 1),), 1, True)
    return padded_2(widened, (("by", 0),), 1, False)


def on_device(
    tracer_one,
    tracer_two,
    east_flow,
    north_flow,
    depth_levels,
    side_mix,
    vert_mix,
    thickness,
    corner_depth,
    diagonal,
):
    levels = lax.broadcasted_iota(jnp.int32, tracer_one.shape, 0)
    wet = (levels < depth_levels[None]).astype(jnp.float32)
    tracers = jnp.stack([tracer_one, tracer_two])
    side = side_mix[:, None, None]
    stacked = jnp.stack(
        [tracer_one, tracer_two, east_flow.astype(jnp.float32), north_flow.astype(jnp.float32), wet]
    )
    widened = padded_2(stacked, (("bx", 3),), 1, True)
    padded = padded_2(widened, (("by", 2),), 1, False)
    tracer_pad = padded[0:2]
    east_cols = padded[2][:, 1:-1, :-1]
    north_rows = padded[3][:, :-1, 1:-1]
    wet_pad = padded[4]
    change = horizontal(tracer_pad, east_cols, north_rows, wet_pad, side)
    updated = wet * (tracers + change + vertical(tracers, wet, vert_mix))
    forcing = jnp.sum(thickness[:, None, None] * (updated[0] - 0.5 * updated[1]), axis=0)
    depth = corner_depth * (depth_levels > 0).astype(jnp.float32)
    depth_ext = block_rim(depth)[:-1, :-1]

    def operate(field):
        return corner_operator(block_rim(field), depth_ext, field, diagonal)

    surface = chron_gear(forcing, operate, device_totals)
    return (updated[0], updated[1], surface)


def solution(mesh):
    return jax.shard_map(
        on_device,
        mesh=mesh,
        in_specs=(
            P(None, "by", "bx"),
            P(None, "by", "bx"),
            P(None, "by", "bx"),
            P(None, "by", "bx"),
            P("by", "bx"),
            P(),
            P(),
            P(),
            P("by", "bx"),
            P("by", "bx"),
        ),
        out_specs=(P(None, "by", "bx"), P(None, "by", "bx"), P("by", "bx")),
        check_vma=False,
    )
```

profile of v0, /device:TPU:0, one launch (start us, length us, event | category | flops | bytes accessed | tf_op | source)
XLA Modules:
  0.0 330.3 jit_solution(2279668869596276225)
XLA Ops:
  21.8 6.1 %collective-permute-start.1 = (f32[5,18,64,1]{2,3,1,0:T(1,128)S(1)}, f32[5,18,64,1]{2,3,1,0:T(1,128)S(1)}, u32[]{:S(2)}, u32[]{:S(2)}) collective-permute-start(f32[5,18,64,1]{2,3,1,0:T(1,128)S(1)} %get-tuple-element.39), channel_id=1, source_target_pairs={{1,0},{2,1},{3,2},{4,3},{5,4},{6,5},{7,6},{0,7},{9,8},{10,9},{11,1... | collective-permute-start | bytes 69128 | tf_op jit(solution)/shard_map/ppermute | solution.py:17
  29.8 4.8 %collective-permute-start.5 = (f32[64,1]{0,1:T(1,128)S(1)}, f32[64,1]{0,1:T(1,128)S(1)}, u32[]{:S(2)}, u32[]{:S(2)}) collective-permute-start(f32[64,1]{0,1:T(1,128)S(1)} %get-tuple-element.59), channel_id=1, source_target_pairs={{1,0},{2,1},{3,2},{4,3},{5,4},{6,5},{7,6},{0,7},{9,8},{10,9},{11,1... | collective-permute-start | bytes 776 | tf_op jit(solution)/shard_map/ppermute | solution.py:17
  37.8 5.5 %pad_maximum_fusion = f32[5,18,64,258]{2,3,1,0:T(8,128)S(1)} fusion(f32[5,18,64,1]{2,3,1,0:T(1,128)S(1)} %collective-permute-done.1, f32[5,18,64,256]{2,3,1,0:T(8,128)} %convert_dynamic-update-slice_fusion.2, f32[5,18,64,1]{2,3,1,0:T(1,128)S(1)} %collective-permute-done), kind=kLoop, calls=%fused_computation | loop fusion | flops 2972160 | bytes 11888640 | tf_op jit(solution)/shard_map/concatenate | solution.py:18
  43.3 9.4 %fusion.31 = (f32[5,18,1,258]{2,3,1,0:T(8,128)}, f32[5,18,1,258]{2,3,1,0:T(8,128)}) fusion(f32[5,18,64,258]{2,3,1,0:T(8,128)S(1)} %pad_maximum_fusion), kind=kLoop, calls=%fused_computation.108 | loop fusion | bytes 371520 | tf_op jit(solution)/shard_map/slice | solution.py:15
  52.8 8.2 %copy.27 = f32[5,18,1,258]{3,2,1,0:T(1,128)S(1)} copy(f32[5,18,1,258]{2,3,1,0:T(8,128)} %get-tuple-element.37) | data formatting | bytes 185760 | tf_op jit(solution)/shard_map/slice | solution.py:14
  62.2 8.2 %copy.28 = f32[5,18,1,258]{3,2,1,0:T(1,128)S(1)} copy(f32[5,18,1,258]{2,3,1,0:T(8,128)} %get-tuple-element.36) | data formatting | bytes 185760 | tf_op jit(solution)/shard_map/slice | solution.py:15
  71.9 5.0 %fusion.8 = f32[2,17,64,256]{2,3,1,0:T(8,128)} fusion(f32[1,18,64,256]{2,3,1,0:T(8,128)} %bitcast.31, f32[1,18,64,256]{2,3,1,0:T(8,128)S(1)} %bitcast.29, f32[17,64,256]{1,2,0:T(8,128)} %slice.316, f32[17]{0:T(128)S(1)} %bitcast.33), kind=kLoop, calls=%fused_computation.26 | loop fusion | flops 2785280 | bytes 5701700 | tf_op jit(solution)/shard_map/mul | solution.py:35
  77.0 6.7 %copy.29 = f32[5,18,1,258]{2,3,1,0:T(8,128)} copy(f32[5,18,1,258]{3,2,1,0:T(1,128)S(1)} %collective-permute-done.2) | data formatting | bytes 185760 | tf_op jit(solution)/shard_map/ppermute | solution.py:16
  83.7 6.8 %copy.30 = f32[5,18,1,258]{2,3,1,0:T(8,128)} copy(f32[5,18,1,258]{3,2,1,0:T(1,128)S(1)} %collective-permute-done.3) | data formatting | bytes 185760 | tf_op jit(solution)/shard_map/ppermute | solution.py:17
  90.5 11.1 %maximum_bitcast_fusion.1 = (f32[18,66,258]{1,2,0:T(8,128)}, f32[18,66,258]{1,2,0:T(8,128)S(1)}, f32[18,66,258]{1,2,0:T(8,128)S(1)}) fusion(f32[5,18,1,258]{2,3,1,0:T(8,128)} %copy.30, f32[5,18,1,258]{2,3,1,0:T(8,128)} %copy.29, f32[5,18,64,1]{2,3,1,0:T(1,128)S(1)} %collective-permute-done.1, f32[5,18,64,256]{2,3,1,0:T(8,128)} %convert_dynamic-update-slice_fusion.2, ...), kind=kLoop, calls=%fused_computation.36 | loop fusion | flops 3678048 | bytes 9808128 | tf_op jit(solution)/shard_map/squeeze | solution.py:113
  105.2 8.1 %slice_multiply_fusion = (f32[18,64,257]{1,2,0:T(8,128)}, f32[18,64,257]{1,2,0:T(8,128)}) fusion(f32[18,66,258]{1,2,0:T(8,128)} %copy-done, f32[18,66,258]{1,2,0:T(8,128)} %get-tuple-element.33), kind=kLoop, calls=%fused_computation.33 | loop fusion | flops 592128 | bytes 5921280 | tf_op jit(solution)/shard_map/mul | solution.py:25
  113.3 7.9 %subtract_multiply_fusion.1 = f32[2,18,65,256]{2,3,1,0:T(8,128)} fusion(f32[5,18,64,1]{2,3,1,0:T(1,128)S(1)} %collective-permute-done.1, f32[5,18,64,256]{2,3,1,0:T(8,128)S(1)} %bitcast.26, f32[5,18,64,1]{2,3,1,0:T(1,128)S(1)} %collective-permute-done, f32[5,18,1,258]{2,3,1,0:T(8,128)S(1)} %bitcast.28, f32[5,18,1,258]{2,3,1,0:T(8,128)} %copy.30, ...), kind=kLoop, calls=%fused_computation.22 | loop fusion | flops 7188480 | bytes 10922472 | tf_op jit(solution)/shard_map/mul | solution.py:30
  121.2 5.1 %subtract_multiply_fusion = f32[2,18,64,257]{2,3,1,0:T(8,128)} fusion(f32[5,18,64,256]{2,3,1,0:T(8,128)S(1)} %bitcast.26, f32[5,18,64,1]{2,3,1,0:T(1,128)S(1)} %collective-permute-done, f32[5,18,64,1]{2,3,1,0:T(1,128)S(1)} %collective-permute-done.1, f32[18,64,257]{1,2,0:T(8,128)} %get-tuple-element.62, f32[18]{0:T(128)S(1)} %copy-done.8, ...), kind=kLoop, calls=%fused_computation.8 | loop fusion | flops 4737024 | bytes 10681416 | tf_op jit(solution)/shard_map/mul | solution.py:26
  126.3 13.1 %fusion.2 = f32[2,18,64,256]{2,3,1,0:T(8,128)S(1)} fusion(f32[1,18,64,256]{2,3,1,0:T(8,128)} %bitcast.30, f32[1,18,64,256]{2,3,1,0:T(8,128)} %bitcast.32, f32[2,18,65,256]{2,3,1,0:T(8,128)} %subtract_multiply_fusion.1, f32[2,18,64,257]{2,3,1,0:T(8,128)} %subtract_multiply_fusion, f32[2,17,64,256]{2,3,1,0:T(8,128)} %fusion.8, f32[18,64,256]{1,2,0:T(8,128)} %copy-done.3), kind=kLoop, calls=%fused_computation.11 | loop fusion | flops 5308416 | bytes 17563648 | tf_op jit(solution)/shard_map/mul | solution.py:117
  149.8 4.2 %collective-permute-start.9 = (f32[1,258]{0,1:T(8,128)S(1)}, f32[1,258]{0,1:T(8,128)S(1)}, u32[]{:S(2)}, u32[]{:S(2)}) collective-permute-start(f32[1,258]{0,1:T(8,128)S(1)} %get-tuple-element.47), channel_id=1, source_target_pairs={{0,8},{8,16},{16,24},{1,9},{9,17},{17,25},{2,10},{10,18},{18,26},{... | collective-permute-start | bytes 3104 | tf_op jit(solution)/shard_map/ppermute | solution.py:16
  154.2 4.8 %collective-permute-start.6 = (f32[1,258]{0,1:T(8,128)S(1)}, f32[1,258]{0,1:T(8,128)S(1)}, u32[]{:S(2)}, u32[]{:S(2)}) collective-permute-start(f32[1,258]{0,1:T(8,128)S(1)} %pad_maximum_fusion.17), channel_id=1, source_target_pairs={{0,8},{8,16},{16,24},{1,9},{9,17},{17,25},{2,10},{10,18},{18,26},{... | collective-permute-start | bytes 3104 | tf_op jit(solution)/shard_map/ppermute | solution.py:16
  160.9 39.0 %all-reduce.4 = (f32[]{:T(128)}, f32[]{:T(128)}) all-reduce(f32[]{:T(128)} %get-tuple-element.14, f32[]{:T(128)} %get-tuple-element.13), channel_id=1, replica_groups=mesh['by'=4,'bx'=8] {'by','bx'}, use_global_device_ids=true, to_apply=%region_2.0 | all-reduce | flops 2 | bytes 16 | tf_op jit(solution)/shard_map/psum | solution.py:83
  201.2 4.2 %collective-permute-start.12 = (f32[64,1]{0,1:T(1,128)S(1)}, f32[64,1]{0,1:T(1,128)S(1)}, u32[]{:S(2)}, u32[]{:S(2)}) collective-permute-start(f32[64,1]{0,1:T(1,128)S(1)} %get-tuple-element.57), channel_id=1, source_target_pairs={{1,0},{2,1},{3,2},{4,3},{5,4},{6,5},{7,6},{0,7},{9,8},{10,9},{11,1... | collective-permute-start | bytes 776 | tf_op jit(solution)/shard_map/ppermute | solution.py:17
  206.8 4.9 %collective-permute-done.11 = f32[64,1]{0,1:T(1,128)S(1)} collective-permute-done((f32[64,1]{0,1:T(1,128)S(1)}, f32[64,1]{0,1:T(1,128)S(1)}, u32[]{:S(2)}, u32[]{:S(2)}) %collective-permute-start.11) | collective-permute-done | bytes 288 | tf_op jit(solution)/shard_map/ppermute | solution.py:16
  218.2 40.4 %all-reduce.3 = (f32[]{:T(128)}, f32[]{:T(128)}) all-reduce(f32[]{:T(128)} %get-tuple-element.12, f32[]{:T(128)} %get-tuple-element.11), channel_id=1, replica_groups=mesh['by'=4,'bx'=8] {'by','bx'}, use_global_device_ids=true, to_apply=%region_6.0 | all-reduce | flops 2 | bytes 16 | tf_op jit(solution)/shard_map/psum | solution.py:83
  263.4 4.3 %collective-permute-start.16 = (f32[64,1]{0,1:T(1,128)S(1)}, f32[64,1]{0,1:T(1,128)S(1)}, u32[]{:S(2)}, u32[]{:S(2)}) collective-permute-start(f32[64,1]{0,1:T(1,128)S(1)} %get-tuple-element.55), channel_id=1, source_target_pairs={{1,0},{2,1},{3,2},{4,3},{5,4},{6,5},{7,6},{0,7},{9,8},{10,9},{11,1... | collective-permute-start | bytes 776 | tf_op jit(solution)/shard_map/ppermute | solution.py:17
  268.9 4.9 %collective-permute-done.15 = f32[64,1]{0,1:T(1,128)S(1)} collective-permute-done((f32[64,1]{0,1:T(1,128)S(1)}, f32[64,1]{0,1:T(1,128)S(1)}, u32[]{:S(2)}, u32[]{:S(2)}) %collective-permute-start.15) | collective-permute-done | bytes 288 | tf_op jit(solution)/shard_map/ppermute | solution.py:16
  278.9 4.2 %slice_bitcast_fusion = (f32[18,64,256]{1,2,0:T(8,128)S(1)}, f32[18,64,256]{1,2,0:T(8,128)}) fusion(f32[2,18,64,256]{2,3,1,0:T(8,128)} %copy-done.1), kind=kLoop, calls=%fused_computation.37 | loop fusion | bytes 4718592 | tf_op jit(solution)/shard_map/squeeze | solution.py:126
  288.7 37.1 %all-reduce.2 = (f32[]{:T(128)}, f32[]{:T(128)}) all-reduce(f32[]{:T(128)} %get-tuple-element.10, f32[]{:T(128)} %get-tuple-element.9), channel_id=1, replica_groups=mesh['by'=4,'bx'=8] {'by','bx'}, use_global_device_ids=true, to_apply=%region_10.0 | all-reduce | flops 2 | bytes 16 | tf_op jit(solution)/shard_map/psum | solution.py:83
  (113 shorter events, 65.4 us)
Async XLA Ops:
  2.5 69.4 %copy-start.2 = (f32[18,64,256]{1,2,0:T(8,128)}, f32[18,64,256]{1,2,0:T(8,128)S(1)}, u32[]{:S(2)}) copy-start(f32[18,64,256]{1,2,0:T(8,128)S(1)} %copy.23) | copy-start | bytes 3538948
  21.8 15.5 %collective-permute-start.1 = (f32[5,18,64,1]{2,3,1,0:T(1,128)S(1)}, f32[5,18,64,1]{2,3,1,0:T(1,128)S(1)}, u32[]{:S(2)}, u32[]{:S(2)}) collective-permute-start(f32[5,18,64,1]{2,3,1,0:T(1,128)S(1)} %get-tuple-element.39), channel_id=1, source_target_pairs={{1,0},{2,1},{3,2},{4,3},{5,4},{6,5},{7,6},{0,7},{9,8},{10,9},{11,1... | collective-permute-start | bytes 69128 | tf_op jit(solution)/shard_map/ppermute | solution.py:17
  27.9 9.9 %collective-permute-start = (f32[5,18,64,1]{2,3,1,0:T(1,128)S(1)}, f32[5,18,64,1]{2,3,1,0:T(1,128)S(1)}, u32[]{:S(2)}, u32[]{:S(2)}) collective-permute-start(f32[5,18,64,1]{2,3,1,0:T(1,128)S(1)} %get-tuple-element.38), channel_id=1, source_target_pairs={{0,1},{1,2},{2,3},{3,4},{4,5},{5,6},{6,7},{7,0},{8,9},{9,10},{10,1... | collective-permute-start | bytes 69128 | tf_op jit(solution)/shard_map/ppermute | solution.py:16
  29.8 124.3 %collective-permute-start.5 = (f32[64,1]{0,1:T(1,128)S(1)}, f32[64,1]{0,1:T(1,128)S(1)}, u32[]{:S(2)}, u32[]{:S(2)}) collective-permute-start(f32[64,1]{0,1:T(1,128)S(1)} %get-tuple-element.59), channel_id=1, source_target_pairs={{1,0},{2,1},{3,2},{4,3},{5,4},{6,5},{7,6},{0,7},{9,8},{10,9},{11,1... | collective-permute-start | bytes 776 | tf_op jit(solution)/shard_map/ppermute | solution.py:17
  60.9 16.1 %collective-permute-start.2 = (f32[5,18,1,258]{3,2,1,0:T(1,128)S(1)}, f32[5,18,1,258]{3,2,1,0:T(1,128)S(1)}, u32[]{:S(2)}, u32[]{:S(2)}) collective-permute-start(f32[5,18,1,258]{3,2,1,0:T(1,128)S(1)} %copy.27), channel_id=1, source_target_pairs={{0,8},{8,16},{16,24},{1,9},{9,17},{17,25},{2,10},{10,18},{18,26},{... | collective-permute-start | bytes 278648 | tf_op jit(solution)/shard_map/ppermute | solution.py:16
  70.4 13.3 %collective-permute-start.3 = (f32[5,18,1,258]{3,2,1,0:T(1,128)S(1)}, f32[5,18,1,258]{3,2,1,0:T(1,128)S(1)}, u32[]{:S(2)}, u32[]{:S(2)}) collective-permute-start(f32[5,18,1,258]{3,2,1,0:T(1,128)S(1)} %copy.28), channel_id=1, source_target_pairs={{8,0},{16,8},{24,16},{9,1},{17,9},{25,17},{10,2},{18,10},{26,18},{... | collective-permute-start | bytes 278648 | tf_op jit(solution)/shard_map/ppermute | solution.py:17
  90.5 22.8 %slice-start.3 = ((s8[12165120]{0:T(1024)(128)(4,1)}), s8[4194304]{0:T(1024)(128)(4,1)S(1)}, s32[]{:S(2)}) async-start(s8[12165120]{0:T(1024)(128)(4,1)} %bitcast.27), calls=%async_computation.3 | async-start | bytes 8388608
  90.5 22.8 %slice-start.4 = ((s8[12165120]{0:T(1024)(128)(4,1)}), s8[4194304]{0:T(1024)(128)(4,1)S(1)}, s32[]{:S(2)}) async-start(s8[12165120]{0:T(1024)(128)(4,1)} %bitcast.27), calls=%async_computation.4 | async-start | bytes 8388608
  101.6 11.6 %slice-start = ((s8[11796480]{0:T(1024)(128)(4,1)}), s8[4194304]{0:T(1024)(128)(4,1)S(1)}, s32[]{:S(2)}) async-start(s8[11796480]{0:T(1024)(128)(4,1)} %bitcast.25), calls=%async_computation | async-start | bytes 8388608
  126.3 15.3 %copy-start.10 = (f32[18]{0:T(128)S(1)}, f32[18]{0:T(128)}, u32[]{:S(2)}) copy-start(f32[18]{0:T(128)} %param.17) | copy-start | bytes 220
  142.1 3.6 %collective-permute-start.8 = (f32[64,1]{0,1:T(1,128)S(1)}, f32[64,1]{0,1:T(1,128)S(1)}, u32[]{:S(2)}, u32[]{:S(2)}) collective-permute-start(f32[64,1]{0,1:T(1,128)S(1)} %get-tuple-element.61), channel_id=1, source_target_pairs={{1,0},{2,1},{3,2},{4,3},{5,4},{6,5},{7,6},{0,7},{9,8},{10,9},{11,1... | collective-permute-start | bytes 776 | tf_op jit(solution)/shard_map/ppermute | solution.py:17
  142.1 6.3 %collective-permute-start.7 = (f32[64,1]{0,1:T(1,128)S(1)}, f32[64,1]{0,1:T(1,128)S(1)}, u32[]{:S(2)}, u32[]{:S(2)}) collective-permute-start(f32[64,1]{0,1:T(1,128)S(1)} %get-tuple-element.60), channel_id=1, source_target_pairs={{0,1},{1,2},{2,3},{3,4},{4,5},{5,6},{6,7},{7,0},{8,9},{9,10},{10,1... | collective-permute-start | bytes 776 | tf_op jit(solution)/shard_map/ppermute | solution.py:16
  144.1 10.0 %collective-permute-start.4 = (f32[64,1]{0,1:T(1,128)S(1)}, f32[64,1]{0,1:T(1,128)S(1)}, u32[]{:S(2)}, u32[]{:S(2)}) collective-permute-start(f32[64,1]{0,1:T(1,128)S(1)} %get-tuple-element.58), channel_id=1, source_target_pairs={{0,1},{1,2},{2,3},{3,4},{4,5},{5,6},{6,7},{7,0},{8,9},{9,10},{10,1... | collective-permute-start | bytes 776 | tf_op jit(solution)/shard_map/ppermute | solution.py:16
  148.5 10.5 %collective-permute-start.10 = (f32[1,258]{0,1:T(8,128)S(1)}, f32[1,258]{0,1:T(8,128)S(1)}, u32[]{:S(2)}, u32[]{:S(2)}) collective-permute-start(f32[1,258]{0,1:T(8,128)S(1)} %get-tuple-element.46), channel_id=1, source_target_pairs={{8,0},{16,8},{24,16},{9,1},{17,9},{25,17},{10,2},{18,10},{26,18},{... | collective-permute-start | bytes 3104 | tf_op jit(solution)/shard_map/ppermute | solution.py:17
  149.8 9.2 %collective-permute-start.9 = (f32[1,258]{0,1:T(8,128)S(1)}, f32[1,258]{0,1:T(8,128)S(1)}, u32[]{:S(2)}, u32[]{:S(2)}) collective-permute-start(f32[1,258]{0,1:T(8,128)S(1)} %get-tuple-element.47), channel_id=1, source_target_pairs={{0,8},{8,16},{16,24},{1,9},{9,17},{17,25},{2,10},{10,18},{18,26},{... | collective-permute-start | bytes 3104 | tf_op jit(solution)/shard_map/ppermute | solution.py:16
  154.2 5.8 %collective-permute-start.6 = (f32[1,258]{0,1:T(8,128)S(1)}, f32[1,258]{0,1:T(8,128)S(1)}, u32[]{:S(2)}, u32[]{:S(2)}) collective-permute-start(f32[1,258]{0,1:T(8,128)S(1)} %pad_maximum_fusion.17), channel_id=1, source_target_pairs={{0,8},{8,16},{16,24},{1,9},{9,17},{17,25},{2,10},{10,18},{18,26},{... | collective-permute-start | bytes 3104 | tf_op jit(solution)/shard_map/ppermute | solution.py:16
  201.2 5.5 %collective-permute-start.12 = (f32[64,1]{0,1:T(1,128)S(1)}, f32[64,1]{0,1:T(1,128)S(1)}, u32[]{:S(2)}, u32[]{:S(2)}) collective-permute-start(f32[64,1]{0,1:T(1,128)S(1)} %get-tuple-element.57), channel_id=1, source_target_pairs={{1,0},{2,1},{3,2},{4,3},{5,4},{6,5},{7,6},{0,7},{9,8},{10,9},{11,1... | collective-permute-start | bytes 776 | tf_op jit(solution)/shard_map/ppermute | solution.py:17
  205.5 6.2 %collective-permute-start.11 = (f32[64,1]{0,1:T(1,128)S(1)}, f32[64,1]{0,1:T(1,128)S(1)}, u32[]{:S(2)}, u32[]{:S(2)}) collective-permute-start(f32[64,1]{0,1:T(1,128)S(1)} %get-tuple-element.56), channel_id=1, source_target_pairs={{0,1},{1,2},{2,3},{3,4},{4,5},{5,6},{6,7},{7,0},{8,9},{9,10},{10,1... | collective-permute-start | bytes 776 | tf_op jit(solution)/shard_map/ppermute | solution.py:16
  211.8 4.3 %collective-permute-start.14 = (f32[1,258]{0,1:T(8,128)S(1)}, f32[1,258]{0,1:T(8,128)S(1)}, u32[]{:S(2)}, u32[]{:S(2)}) collective-permute-start(f32[1,258]{0,1:T(8,128)S(1)} %get-tuple-element.44), channel_id=1, source_target_pairs={{8,0},{16,8},{24,16},{9,1},{17,9},{25,17},{10,2},{18,10},{26,18},{... | collective-permute-start | bytes 3104 | tf_op jit(solution)/shard_map/ppermute | solution.py:17
  213.1 4.0 %collective-permute-start.13 = (f32[1,258]{0,1:T(8,128)S(1)}, f32[1,258]{0,1:T(8,128)S(1)}, u32[]{:S(2)}, u32[]{:S(2)}) collective-permute-start(f32[1,258]{0,1:T(8,128)S(1)} %get-tuple-element.45), channel_id=1, source_target_pairs={{0,8},{8,16},{16,24},{1,9},{9,17},{17,25},{2,10},{10,18},{18,26},{... | collective-permute-start | bytes 3104 | tf_op jit(solution)/shard_map/ppermute | solution.py:16
  263.4 5.6 %collective-permute-start.16 = (f32[64,1]{0,1:T(1,128)S(1)}, f32[64,1]{0,1:T(1,128)S(1)}, u32[]{:S(2)}, u32[]{:S(2)}) collective-permute-start(f32[64,1]{0,1:T(1,128)S(1)} %get-tuple-element.55), channel_id=1, source_target_pairs={{1,0},{2,1},{3,2},{4,3},{5,4},{6,5},{7,6},{0,7},{9,8},{10,9},{11,1... | collective-permute-start | bytes 776 | tf_op jit(solution)/shard_map/ppermute | solution.py:17
  267.6 6.2 %collective-permute-start.15 = (f32[64,1]{0,1:T(1,128)S(1)}, f32[64,1]{0,1:T(1,128)S(1)}, u32[]{:S(2)}, u32[]{:S(2)}) collective-permute-start(f32[64,1]{0,1:T(1,128)S(1)} %get-tuple-element.54), channel_id=1, source_target_pairs={{0,1},{1,2},{2,3},{3,4},{4,5},{5,6},{6,7},{7,0},{8,9},{9,10},{10,1... | collective-permute-start | bytes 776 | tf_op jit(solution)/shard_map/ppermute | solution.py:16
  274.6 13.0 %collective-permute-start.18 = (f32[1,258]{0,1:T(8,128)}, f32[1,258]{0,1:T(8,128)S(1)}, u32[]{:S(2)}, u32[]{:S(2)}) collective-permute-start(f32[1,258]{0,1:T(8,128)} %get-tuple-element.42), channel_id=1, source_target_pairs={{8,0},{16,8},{24,16},{9,1},{17,9},{25,17},{10,2},{18,10},{26,18},{... | collective-permute-start | bytes 3104 | tf_op jit(solution)/shard_map/ppermute | solution.py:17
  275.9 11.8 %collective-permute-start.17 = (f32[1,258]{0,1:T(8,128)S(1)}, f32[1,258]{0,1:T(8,128)S(1)}, u32[]{:S(2)}, u32[]{:S(2)}) collective-permute-start(f32[1,258]{0,1:T(8,128)S(1)} %get-tuple-element.43), channel_id=1, source_target_pairs={{0,8},{8,16},{16,24},{1,9},{9,17},{17,25},{2,10},{10,18},{18,26},{... | collective-permute-start | bytes 3104 | tf_op jit(solution)/shard_map/ppermute | solution.py:16
  (12 other events, 71.5 us)
where the time goes:
time: 333 us; the launch traced here: 330 us
  blocking collectives  116 us (35%)
  local copies, waits for them, and re-layouts  71.5 us (21%)
  other arithmetic  69.9 us (21%)
  starting transfers between devices  43.2 us (13%)
  waiting for transfers between devices  18.4 us (6%)
  between operations  10.9 us (3%)
    psum x3, blocking collectives, device_totals(): return lax.psum((jnp.sum(first), jnp.sum(second)), ('by', 'bx'))  116 us
    ppermute x9, starting transfers between devices, padded_2(): after = lax.ppermute(first, axis, down)  24.8 us
    unnamed x46, local copies, waits for them, and re-layouts  24.2 us
    slice x5, local copies, waits for them, and re-layouts, padded_2(): first = lax.slice_in_dim(shard, 0, width, axis=dim)  18.5 us
    ppermute x10, starting transfers between devices, padded_2(): before = lax.ppermute(last, axis, up)  18.5 us
    ppermute x10, waiting for transfers between devices, padded_2(): before = lax.ppermute(last, axis, up)  14.4 us
    mul x1, other arithmetic, on_device(): updated = wet * (tracers + change + vertical(tracers, wet, vert_mix))  13.1 us
    squeeze x1, other arithmetic, on_device(): east_cols = padded[2][:, 1:-1, :-1]  11.1 us
  transfers between devices with their start and end apart: 19, of which 8 were waited for; matrix products, arithmetic and copies ran while one was open for 34% of the time, Pallas kernels for 0%

commit v1 on v0

v1 whole, which is shorter than its diff:
```python
import functools

import jax
import jax.numpy as jnp
from jax import lax
from jax.experimental import pallas as pl
from jax.experimental.pallas import tpu as pltpu
from jax.sharding import PartitionSpec as P

ITERS = 3
SHIFT = 3.0
CHUNK = 16
LANES = 128
MESH = pl.DeviceIdType.MESH
f32 = jnp.float32
SIDES = ((1, 0), (-1, 0), (0, 1), (0, -1), (1, 1), (1, -1), (-1, 1), (-1, -1))


def iterate_weights(moments):
    def add(a, b, scale):
        longer = max(len(a), len(b))
        out = []
        for n in range(longer):
            if n >= len(a):
                out.append(scale * b[n])
            elif n >= len(b):
                out.append(a[n])
            else:
                out.append(a[n] + scale * b[n])
        return out

    def operate(a):
        shifted = [SHIFT * x for x in a] + [None]
        for n, x in enumerate(a):
            shifted[n + 1] = x if shifted[n + 1] is None else shifted[n + 1] + x
        return shifted

    def dot(a, b):
        total = None
        for i, x in enumerate(a):
            for j, y in enumerate(b):
                term = x * y * moments[i + j]
                total = term if total is None else total + term
        return total

    residual = [jnp.ones_like(moments[0])]
    image = operate(residual)
    now = dot(residual, residual)
    alpha = now / dot(residual, image)
    direction, along = residual, image
    surface = [jnp.zeros_like(moments[0])]
    for step in range(ITERS):
        surface = add(surface, direction, alpha)
        if step + 1 < ITERS:
            residual = add(residual, along, -alpha)
            image = operate(residual)
            new = dot(residual, residual)
            product = dot(residual, image)
            ratio = new / now
            alpha = new / (product - ratio * new / alpha)
            direction = add(residual, direction, ratio)
            along = add(image, along, ratio)
            now = new
    return surface


def kernel(
    nby, nbx, nlev,
    side, vert, thick, t1h, t2h, uh, vh, levh, cdh, dgh,
    o1h, o2h, surf,
    t, u, v, levi, o, row_up, row_dn, got_dn, got_up, col_rt, col_lf, got_lf, got_rt,
    flx, fw, fld, h_up, h_dn, h_rt, h_lf, h_cn, v1r, v2r, mom, gath,
    load_sem, out_sem, send_a, recv_a, send_b, recv_b, send_c, recv_c, gsend, grecv,
):
    by, bx = lax.axis_index("by"), lax.axis_index("bx")
    total = nby * nbx
    me = by * nbx + bx
    ny, nx = fld.shape[1], fld.shape[2]

    loads = [
        pltpu.make_async_copy(levh, levi, load_sem.at[4]),
        pltpu.make_async_copy(cdh, fld.at[1], load_sem.at[5]),
        pltpu.make_async_copy(dgh, fld.at[2], load_sem.at[6]),
        pltpu.make_async_copy(t1h, t.at[0], load_sem.at[0]),
        pltpu.make_async_copy(t2h, t.at[1], load_sem.at[1]),
        pltpu.make_async_copy(uh, u, load_sem.at[2]),
        pltpu.make_async_copy(vh, v, load_sem.at[3]),
    ]
    for copy in loads:
        copy.start()

    def other(off):
        who = lax.rem(me + off, total)
        return (who // nbx, lax.rem(who, nbx))

    barrier = pltpu.get_barrier_semaphore()

    def greet(off, _):
        pl.semaphore_signal(barrier, inc=1, device_id=other(off), device_id_type=MESH)
        return 0

    lax.fori_loop(1, total, greet, 0)

    def neighbour(dy, dx):
        return (lax.rem(by + dy + nby, nby), lax.rem(bx + dx + nbx, nbx))

    up_ok = jnp.where(by < nby - 1, 1.0, 0.0).astype(f32)
    dn_ok = jnp.where(by > 0, 1.0, 0.0).astype(f32)

    for copy in loads[:3]:
        copy.wait()
    levels = levi[...]
    levf = levels.astype(f32)
    fld[1] = fld[1] * jnp.where(levels > 0, 0.5, 0.0).astype(f32)
    fld[2] = fld[2] - SHIFT
    for copy in loads[3:]:
        copy.wait()

    lane = lax.broadcasted_iota(jnp.int32, (ny, LANES), 1)
    row_up[pl.ds(72, 8), :] = jnp.broadcast_to(levf[ny - 1 : ny], (8, nx))
    row_dn[pl.ds(72, 8), :] = jnp.broadcast_to(levf[0:1], (8, nx))

    def pack(k, carry):
        right, left = carry
        for c in range(2):
            row_up[pl.ds(24 * c + k, 1), :] = t[c, k, ny - 1 : ny, :]
            row_dn[pl.ds(24 * c + k, 1), :] = t[c, k, 0:1, :]
            place = 32 * c + k
            right = jnp.where(lane == place, pltpu.roll(t[c, k, :, nx - LANES :], place + 1, 1), right)
            left = jnp.where(lane == place, pltpu.roll(t[c, k, :, :LANES], place, 1), left)
        row_up[pl.ds(48 + k, 1), :] = v[k, ny - 16 :, :].astype(f32)[15:16]
        right = jnp.where(lane == 64 + k, pltpu.roll(u[k, :, nx - LANES :].astype(f32), 65 + k, 1), right)
        return right, left

    first = jnp.zeros((ny, LANES), f32)
    right, left = lax.fori_loop(0, nlev, pack, (first, first))
    col_rt[...] = jnp.where(lane == 96, pltpu.roll(levf[:, nx - LANES :], 97, 1), right)
    col_lf[...] = jnp.where(lane == 96, pltpu.roll(levf[:, :LANES], 96, 1), left)

    pl.semaphore_wait(barrier, total - 1)

    def send(src, dst, ssem, rsem, to):
        copy = pltpu.make_async_remote_copy(
            src_ref=src, dst_ref=dst, send_sem=ssem, recv_sem=rsem, device_id=to, device_id_type=MESH
        )
        copy.start()
        return copy

    edge = [
        send(row_up, got_dn, send_a.at[0], recv_a.at[0], neighbour(1, 0)),
        send(row_dn, got_up, send_a.at[1], recv_a.at[1], neighbour(-1, 0)),
        send(col_rt, got_lf, send_a.at[2], recv_a.at[2], neighbour(0, 1)),
        send(col_lf, got_rt, send_a.at[3], recv_a.at[3], neighbour(0, -1)),
    ]

    def rim(which, ssem, rsem):
        copies = []
        for n, (dy, dx) in enumerate(SIDES):
            rows = pl.ds(0, ny) if dy == 0 else (pl.ds(ny - 8, 8) if dy > 0 else pl.ds(0, 8))
            cols = pl.ds(0, nx) if dx == 0 else (pl.ds(nx - LANES, LANES) if dx > 0 else pl.ds(0, LANES))
            place = {0: h_dn, 1: h_up, 2: h_lf, 3: h_rt}.get(n)
            dst = h_cn.at[n - 4, which] if place is None else place.at[which]
            copies.append(send(fld.at[which, rows, cols], dst, ssem.at[n], rsem.at[n], neighbour(dy, dx)))
        return copies

    rim_fixed = rim(pl.ds(1, 2), send_b, recv_b)

    for copy in edge:
        copy.wait_recv()

    k_sub = lax.broadcasted_iota(jnp.int32, (24, nx), 0)
    k_lane = lax.rem(lane, 32)
    side_sub = jnp.zeros((24, nx), f32)
    side_lane = jnp.zeros((ny, LANES), f32)
    for k in range(nlev):
        side_sub = jnp.where(k_sub == k, side[k], side_sub)
        side_lane = jnp.where(k_lane == k, side[k], side_lane)
    lowest = jnp.minimum(got_dn[72:73, :] * dn_ok, levf[0:1])
    open_dn = k_sub.astype(f32) < lowest
    half = 0.5 * got_dn[48:72, :]
    for c in range(2):
        flux = (half + side_sub) * got_dn[24 * c : 24 * c + 24, :] + (half - side_sub) * row_dn[24 * c : 24 * c + 24, :]
        flx[c] = jnp.where(open_dn, flux, 0.0)
    came = got_lf[...]
    half = 0.5 * jnp.where(lane < 32, pltpu.roll(came, 64, 1), pltpu.roll(came, 96, 1))
    lowest = jnp.minimum(came[:, 96:97], levf[:, 0:1])
    flux = (half + side_lane) * came + (half - side_lane) * col_lf[...]
    fw[...] = jnp.where(k_lane.astype(f32) < lowest, flux, 0.0)

    lane_c = lax.broadcasted_iota(jnp.int32, (CHUNK, LANES), 1)
    sub_c = lax.broadcasted_iota(jnp.int32, (CHUNK, nx), 0)

    def at_last_lane(whole, tile):
        return jnp.concatenate([whole[:, : nx - LANES], jnp.where(lane_c == LANES - 1, tile, whole[:, nx - LANES :])], axis=1)

    def at_first_lane(whole, tile):
        return jnp.concatenate([jnp.where(lane_c == 0, tile, whole[:, :LANES]), whole[:, LANES:]], axis=1)

    for r in range(0, ny, CHUNK):
        rows = slice(r, r + CHUNK)
        lev = levf[rows]
        lev_rt = at_last_lane(pltpu.roll(lev, nx - 1, 1), jnp.broadcast_to(got_rt[rows, 96:97], (CHUNK, LANES)))
        above = levf[r + CHUNK : r + CHUNK + 1] if r + CHUNK < ny else got_up[72:73, :] * up_ok
        lev_up = jnp.where(sub_c == CHUNK - 1, above, pltpu.roll(lev, CHUNK - 1, 0))
        open_e = jnp.minimum(lev, lev_rt)
        open_n = jnp.minimum(lev, lev_up)

        def level(k, carry, r=r, rows=rows, lev=lev, open_e=open_e, open_n=open_n):
            falls, force = carry
            kf = k.astype(f32)
            s = side[k]
            hu = 0.5 * u[k, rows, :].astype(f32)
            hv = 0.5 * v[k, rows, :].astype(f32)
            in_e, in_n = kf < open_e, kf < open_n
            pe, qe = jnp.where(in_e, hu + s, 0.0), jnp.where(in_e, hu - s, 0.0)
            pn, qn = jnp.where(in_n, hv + s, 0.0), jnp.where(in_n, hv - s, 0.0)
            wet = kf < lev
            fall_w = jnp.where(kf + 1.0 < lev, vert[k], 0.0)
            below = jnp.minimum(k + 1, nlev - 1)
            rt, lf = got_rt[rows, :], fw[rows, :]
            news, next_falls = [], []
            for c in range(2):
                here = t[c, k, rows, :]
                right = at_last_lane(pltpu.roll(here, nx - 1, 1), pltpu.roll(rt, 127 - 32 * c - k, 1))
                top = t[c, k, r + CHUNK : r + CHUNK + 1, :] if r + CHUNK < ny else got_up[pl.ds(24 * c + k, 1), :]
                upper = jnp.where(sub_c == CHUNK - 1, top, pltpu.roll(here, CHUNK - 1, 0))
                east = pe * here + qe * right
                north = pn * here + qn * upper
                west = at_first_lane(pltpu.roll(east, 1, 1), pltpu.roll(lf, lax.rem(128 - 32 * c - k, 128), 1))
                south = jnp.where(sub_c == 0, flx[c, pl.ds(k, 1), :], pltpu.roll(north, 1, 0))
                if r + CHUNK < ny:
                    flx[c, pl.ds(k, 1), :] = north[CHUNK - 1 :]
                fall = fall_w * (t[c, below, rows, :] - here)
                new = jnp.where(wet, here + (west - east) + (south - north) + (fall - falls[c]), 0.0)
                o[c, k, rows, :] = new
                news.append(new)
                next_falls.append(fall)
            force = force + thick[k] * (news[0] - 0.5 * news[1])
            return tuple(next_falls), force

        zero = jnp.zeros((CHUNK, nx), f32)
        _, force = lax.fori_loop(0, nlev, level, ((zero, zero), zero))
        fld[0, rows, :] = force

    outs = [
        pltpu.make_async_copy(o.at[0], o1h, out_sem.at[0]),
        pltpu.make_async_copy(o.at[1], o2h, out_sem.at[1]),
    ]
    rim_force = rim(0, send_c, recv_c)
    for copy in outs:
        copy.start()

    sub8 = lax.broadcasted_iota(jnp.int32, (8, nx), 0) < 4
    sub8c = sub8[:, :LANES]
    lane8 = lax.broadcasted_iota(jnp.int32, (8, LANES), 1) < 64
    lane64 = lane < 64
    row = lax.broadcasted_iota(jnp.int32, (ny + 8, nx + LANES), 0)
    mask = jnp.where(row < ny, 1.0, jnp.where(row < ny + 4, up_ok, dn_ok)).astype(f32)

    def widened(n):
        beside = jnp.where(lane64, h_rt[n], h_lf[n])
        ends = jnp.where(sub8, h_up[n], h_dn[n])
        corner = jnp.where(
            sub8c, jnp.where(lane8, h_cn[3, n], h_cn[2, n]), jnp.where(lane8, h_cn[1, n], h_cn[0, n])
        )
        top = jnp.concatenate([fld[n], beside], axis=1)
        bottom = jnp.concatenate([ends, corner], axis=1)
        return jnp.concatenate([top, bottom], axis=0) * mask

    for copy in rim_fixed:
        copy.wait_recv()
    depth, diag = widened(1), widened(2)
    for copy in rim_force:
        copy.wait_recv()
    tall, wide = ny + 8, nx + LANES

    def operate(a):
        b = pltpu.roll(a, wide - 1, 1)
        cc = pltpu.roll(a, tall - 1, 0)
        d = pltpu.roll(b, tall - 1, 0)
        p = depth * (d - a)
        q = depth * (b - cc)
        return (diag * a - p + pltpu.roll(q, 1, 1) + pltpu.roll(pltpu.roll(p, 1, 1) - q, 1, 0)) * mask

    def moment(a, b):
        prod = a[:ny, :nx] * b[:ny, :nx]
        prod = jnp.sum(prod.reshape(ny // 8, 8, nx), axis=0)
        prod = sum(prod[:, n : n + LANES] for n in range(0, nx, LANES))
        return jnp.sum(prod, axis=0, keepdims=True)

    w0 = widened(0)
    w1 = operate(w0)
    w2 = operate(w1)
    w3 = operate(w2)
    v1r[...] = w1[:ny, :nx]
    v2r[...] = w2[:ny, :nx]
    pairs = ((w0, w0), (w0, w1), (w1, w1), (w1, w2), (w2, w2), (w2, w3))
    mom[...] = jnp.concatenate([moment(a, b) for a, b in pairs] + [jnp.zeros((2, LANES), f32)], axis=0)

    def tell(off, _):
        send(mom, gath.at[me], gsend, grecv, other(off))
        return 0

    lax.fori_loop(1, total, tell, 0)
    gath[me] = mom[...]
    for copy in edge + rim_fixed + rim_force:
        copy.wait_send()
    for copy in outs:
        copy.wait()
    every = gath.at[pl.ds(0, total - 1)]
    pltpu.make_async_copy(every, every, grecv).wait()
    sums = jnp.sum(jnp.sum(gath[...], axis=0), axis=1, keepdims=True)
    weights = iterate_weights([sums[n : n + 1] for n in range(6)])
    surf[...] = weights[0] * fld[0] + weights[1] * v1r[...] + weights[2] * v2r[...]
    pltpu.make_async_copy(every, every, gsend).wait()


def on_device(nby, nbx, t1, t2, u, v, lev, side, vert, thick, cd, dg):
    nlev, ny, nx = t1.shape
    anywhere = pl.BlockSpec(memory_space=pl.ANY)
    scalars = pl.BlockSpec(memory_space=pltpu.SMEM)
    vmem = pltpu.VMEM
    dma = pltpu.SemaphoreType.DMA
    cells = nlev * ny * nx
    return pl.pallas_call(
        functools.partial(kernel, nby, nbx, nlev),
        out_shape=(
            jax.ShapeDtypeStruct(t1.shape, f32),
            jax.ShapeDtypeStruct(t1.shape, f32),
            jax.ShapeDtypeStruct((ny, nx), f32),
        ),
        in_specs=[scalars] * 3 + [anywhere] * 7,
        out_specs=(anywhere, anywhere, pl.BlockSpec(memory_space=vmem)),
        scratch_shapes=[
            vmem((2, nlev, ny, nx), f32),
            vmem((nlev, ny, nx), u.dtype),
            vmem((nlev, ny, nx), v.dtype),
            vmem((ny, nx), jnp.int32),
            vmem((2, nlev, ny, nx), f32),
            vmem((80, nx), f32),
            vmem((80, nx), f32),
            vmem((80, nx), f32),
            vmem((80, nx), f32),
            vmem((ny, LANES), f32),
            vmem((ny, LANES), f32),
            vmem((ny, LANES), f32),
            vmem((ny, LANES), f32),
            vmem((2, 24, nx), f32),
            vmem((ny, LANES), f32),
            vmem((3, ny, nx), f32),
            vmem((3, 8, nx), f32),
            vmem((3, 8, nx), f32),
            vmem((3, ny, LANES), f32),
            vmem((3, ny, LANES), f32),
            vmem((4, 3, 8, LANES), f32),
            vmem((ny, nx), f32),
            vmem((ny, nx), f32),
            vmem((8, LANES), f32),
            vmem((nby * nbx, 8, LANES), f32),
            dma((7,)),
            dma((2,)),
            dma((4,)),
            dma((4,)),
            dma((8,)),
            dma((8,)),
            dma((8,)),
            dma((8,)),
            dma,
            dma,
        ],
        compiler_params=pltpu.CompilerParams(
            collective_id=0, has_side_effects=True, vmem_limit_bytes=40 * 2**20
        ),
        cost_estimate=pl.CostEstimate(flops=60 * cells, bytes_accessed=20 * cells, transcendentals=0),
    )(side, vert, thick, t1, t2, u, v, lev, cd, dg)


def solution(mesh):
    def body(t1, t2, u, v, lev, side, vert, thick, cd, dg):
        return on_device(mesh.shape["by"], mesh.shape["bx"], t1, t2, u, v, lev, side, vert, thick, cd, dg)

    block, plane = P(None, "by", "bx"), P("by", "bx")
    return jax.shard_map(
        body,
        mesh=mesh,
        in_specs=(block, block, block, block, plane, P(), P(), P(), plane, plane),
        out_specs=(block, block, plane),
        check_vma=False,
    )
```

time: 333 us -> 49.7 us (0.15)
  blocking collectives: 116 us -> 0 us
  other arithmetic: 69.9 us -> 0 us
  local copies, waits for them, and re-layouts: 71.5 us -> 11.8 us
  starting transfers between devices: 43.2 us -> 0 us
  Pallas kernels: 0 us -> 36.8 us
  waiting for transfers between devices: 18.4 us -> 0 us
  between operations: 10.9 us -> 0.66 us
    psum x3 -> x0, blocking collectives: 116 us -> none  [device_totals(): return lax.psum((jnp.sum(first), jnp.sum(second)), ('by', 'bx'))]
    mul x7 -> x0, other arithmetic: 43.3 us -> none  [the longest x1 13.1 us: on_device(): updated = wet * (tracers + change + vertical(tracers, wet, vert_mix))]
    ppermute x19 -> x0, starting transfers between devices: 43.2 us -> none  [the longest x9 24.8 us: padded_2(): after = lax.ppermute(first, axis, down)]
    pallas_call x0 -> x1, Pallas kernels: none -> 36.8 us  [on_device(): pl.pallas_call(functools.partial(kernel, nby, nbx, nlev), out_shape=(jax....]
    slice x12 -> x0, local copies, waits for them, and re-layouts: 29.5 us -> none  [the longest x5 18.5 us: padded_2(): first = lax.slice_in_dim(shard, 0, width, axis=dim)]
    ppermute x19 -> x0, waiting for transfers between devices: 18.4 us -> none  [the longest x10 14.4 us: padded_2(): before = lax.ppermute(last, axis, up)]
    ppermute x2 -> x0, local copies, waits for them, and re-layouts: 13.5 us -> none  [the longest x1 6.8 us: padded_2(): after = lax.ppermute(first, axis, down)]
    unnamed x46 -> x23, local copies, waits for them, and re-layouts: 24.2 us -> 11.8 us
  transfers between devices with their start and end apart: 19 -> 0, of which waited for: 8 -> 0; matrix products, arithmetic and copies ran while one was open for 34% -> 0% of each run, Pallas kernels for 0% -> 0%
where the time goes in v1:
time: 49.7 us; the launch traced here: 49.3 us
  Pallas kernels  36.8 us (74%)
  local copies, waits for them, and re-layouts  11.8 us (24%)
  between operations  0.66 us (1%)
    pallas_call x1, Pallas kernels, on_device(): pl.pallas_call(functools.partial(kernel, nby, nbx, nlev), out_shape=(jax....  36.8 us
    unnamed x23, local copies, waits for them, and re-layouts  11.8 us

profile of v1, /device:TPU:0, one launch (start us, length us, event | category | flops | bytes accessed | tf_op | source)
XLA Modules:
  0.0 49.3 jit_solution(6050640848050591617)
XLA Ops:
  0.6 0.0 copy-start
  0.6 1.3 %copy-done = f32[18,64,256]{2,1,0:T(8,128)S(1)} copy-done((f32[18,64,256]{2,1,0:T(8,128)S(1)}, f32[18,64,256]{2,1,0:T(8,128)}, u32[]{:S(2)}) %copy-start) | copy-done | bytes 1179672
  1.9 0.0 copy-start.1
  1.9 1.3 %copy-done.1 = f32[18,64,256]{2,1,0:T(8,128)S(1)} copy-done((f32[18,64,256]{2,1,0:T(8,128)S(1)}, f32[18,64,256]{2,1,0:T(8,128)}, u32[]{:S(2)}) %copy-start.1) | copy-done | bytes 1179672
  3.2 0.0 copy-start.2
  3.2 1.1 %copy-done.2 = bf16[18,64,256]{2,1,0:T(8,128)(2,1)S(1)} copy-done((bf16[18,64,256]{2,1,0:T(8,128)(2,1)S(1)}, bf16[18,64,256]{2,1,0:T(8,128)(2,1)}, u32[]{:S(2)}) %copy-start.2) | copy-done | bytes 589848
  4.2 0.0 copy-start.3
  4.2 1.1 %copy-done.3 = bf16[18,64,256]{2,1,0:T(8,128)(2,1)S(1)} copy-done((bf16[18,64,256]{2,1,0:T(8,128)(2,1)S(1)}, bf16[18,64,256]{2,1,0:T(8,128)(2,1)}, u32[]{:S(2)}) %copy-start.3) | copy-done | bytes 589848
  5.3 0.0 copy-start.4
  5.3 0.8 %copy-done.4 = s32[64,256]{1,0:T(8,128)S(1)} copy-done((s32[64,256]{1,0:T(8,128)S(1)}, s32[64,256]{1,0:T(8,128)}, u32[]{:S(2)}) %copy-start.4) | copy-done | bytes 65560
  6.1 0.0 copy-start.5
  6.1 0.8 %copy-done.5 = f32[64,256]{1,0:T(8,128)S(1)} copy-done((f32[64,256]{1,0:T(8,128)S(1)}, f32[64,256]{1,0:T(8,128)}, u32[]{:S(2)}) %copy-start.5) | copy-done | bytes 65560
  7.0 0.0 copy-start.6
  7.0 0.8 %copy-done.6 = f32[64,256]{1,0:T(8,128)S(1)} copy-done((f32[64,256]{1,0:T(8,128)S(1)}, f32[64,256]{1,0:T(8,128)}, u32[]{:S(2)}) %copy-start.6) | copy-done | bytes 65560
  7.8 0.0 copy-start.7
  7.8 0.7 %copy-done.7 = f32[18]{0:T(128)S(1)} copy-done((f32[18]{0:T(128)S(1)}, f32[18]{0:T(128)}, u32[]{:S(2)}) %copy-start.7) | copy-done | bytes 96
  8.5 0.0 copy-start.8
  8.5 0.7 %copy-done.8 = f32[18]{0:T(128)S(1)} copy-done((f32[18]{0:T(128)S(1)}, f32[18]{0:T(128)}, u32[]{:S(2)}) %copy-start.8) | copy-done | bytes 96
  9.1 0.0 copy-start.9
  9.1 0.7 %copy-done.9 = f32[18]{0:T(128)S(1)} copy-done((f32[18]{0:T(128)S(1)}, f32[18]{0:T(128)}, u32[]{:S(2)}) %copy-start.9) | copy-done | bytes 96
  9.8 36.8 %shard_map.121 = (f32[18,64,256]{2,1,0:T(8,128)S(1)}, f32[18,64,256]{2,1,0:T(8,128)S(1)}, f32[64,256]{1,0:T(8,128)S(1)}) custom-call(f32[18]{0:T(128)S(1)} %copy-done.7, f32[18]{0:T(128)S(1)} %copy-done.8, f32[18]{0:T(128)S(1)} %copy-done.9, f32[18,64,256]{2,1,0:T(8,128)S(1)} %copy-done, f32[18,64,256]{2,1,0:T(8,128)S(1)} %copy-done.1, ...), custom_call_target="tpu_custom_call" | custom-call | flops 17694720 | bytes 5898240 | tf_op jit(solution)/shard_map/pallas_call | solution.py:325
  46.6 1.0 %copy.16 = f32[18,64,256]{2,1,0:T(8,128)} copy(f32[18,64,256]{2,1,0:T(8,128)S(1)} %get-tuple-element.6) | data formatting | bytes 2359296
  47.6 1.0 %copy.17 = f32[18,64,256]{2,1,0:T(8,128)} copy(f32[18,64,256]{2,1,0:T(8,128)S(1)} %get-tuple-element.7) | data formatting | bytes 2359296
  48.6 0.6 %copy.18 = f32[64,256]{1,0:T(8,128)} copy(f32[64,256]{1,0:T(8,128)S(1)} %get-tuple-element.8) | data formatting | bytes 131072
Async XLA Ops:
  0.6 1.3 %copy-start = (f32[18,64,256]{2,1,0:T(8,128)S(1)}, f32[18,64,256]{2,1,0:T(8,128)}, u32[]{:S(2)}) copy-start(f32[18,64,256]{2,1,0:T(8,128)} %t1h.1) | copy-start | bytes 3538948
  1.9 1.3 %copy-start.1 = (f32[18,64,256]{2,1,0:T(8,128)S(1)}, f32[18,64,256]{2,1,0:T(8,128)}, u32[]{:S(2)}) copy-start(f32[18,64,256]{2,1,0:T(8,128)} %t2h.1) | copy-start | bytes 3538948
  3.2 1.1 %copy-start.2 = (bf16[18,64,256]{2,1,0:T(8,128)(2,1)S(1)}, bf16[18,64,256]{2,1,0:T(8,128)(2,1)}, u32[]{:S(2)}) copy-start(bf16[18,64,256]{2,1,0:T(8,128)(2,1)} %uh.1) | copy-start | bytes 1769476
  4.2 1.1 %copy-start.3 = (bf16[18,64,256]{2,1,0:T(8,128)(2,1)S(1)}, bf16[18,64,256]{2,1,0:T(8,128)(2,1)}, u32[]{:S(2)}) copy-start(bf16[18,64,256]{2,1,0:T(8,128)(2,1)} %vh.1) | copy-start | bytes 1769476
  5.3 0.8 %copy-start.4 = (s32[64,256]{1,0:T(8,128)S(1)}, s32[64,256]{1,0:T(8,128)}, u32[]{:S(2)}) copy-start(s32[64,256]{1,0:T(8,128)} %levh.1) | copy-start | bytes 196612
  6.1 0.8 %copy-start.5 = (f32[64,256]{1,0:T(8,128)S(1)}, f32[64,256]{1,0:T(8,128)}, u32[]{:S(2)}) copy-start(f32[64,256]{1,0:T(8,128)} %cdh.1) | copy-start | bytes 196612
  7.0 0.8 %copy-start.6 = (f32[64,256]{1,0:T(8,128)S(1)}, f32[64,256]{1,0:T(8,128)}, u32[]{:S(2)}) copy-start(f32[64,256]{1,0:T(8,128)} %dgh.1) | copy-start | bytes 196612
  7.8 0.7 %copy-start.7 = (f32[18]{0:T(128)S(1)}, f32[18]{0:T(128)}, u32[]{:S(2)}) copy-start(f32[18]{0:T(128)} %side.1) | copy-start | bytes 220
  8.5 0.7 %copy-start.8 = (f32[18]{0:T(128)S(1)}, f32[18]{0:T(128)}, u32[]{:S(2)}) copy-start(f32[18]{0:T(128)} %vert.1) | copy-start | bytes 220
  9.1 0.7 %copy-start.9 = (f32[18]{0:T(128)S(1)}, f32[18]{0:T(128)}, u32[]{:S(2)}) copy-start(f32[18]{0:T(128)} %thick.1) | copy-start | bytes 220

commit v2 on v1

v2 whole, which is shorter than its diff:
```python
import functools

import jax
import jax.numpy as jnp
from jax import lax
from jax.experimental import pallas as pl
from jax.experimental.pallas import tpu as pltpu
from jax.sharding import PartitionSpec as P

ITERS = 3
SHIFT = 3.0
CHUNK = 16
UNROLL = 2
VMEM_MIB = 62
LANES = 128
MESH = pl.DeviceIdType.MESH
f32 = jnp.float32
SIDES = ((1, 0), (-1, 0), (0, 1), (0, -1), (1, 1), (1, -1), (-1, 1), (-1, -1))


def iterate_weights(moments):
    def add(a, b, scale):
        longer = max(len(a), len(b))
        out = []
        for n in range(longer):
            if n >= len(a):
                out.append(scale * b[n])
            elif n >= len(b):
                out.append(a[n])
            else:
                out.append(a[n] + scale * b[n])
        return out

    def operate(a):
        shifted = [SHIFT * x for x in a] + [None]
        for n, x in enumerate(a):
            shifted[n + 1] = x if shifted[n + 1] is None else shifted[n + 1] + x
        return shifted

    def dot(a, b):
        total = None
        for i, x in enumerate(a):
            for j, y in enumerate(b):
                term = x * y * moments[i + j]
                total = term if total is None else total + term
        return total

    residual = [jnp.ones_like(moments[0])]
    image = operate(residual)
    now = dot(residual, residual)
    alpha = now / dot(residual, image)
    direction, along = residual, image
    surface = [jnp.zeros_like(moments[0])]
    for step in range(ITERS):
        surface = add(surface, direction, alpha)
        if step + 1 < ITERS:
            residual = add(residual, along, -alpha)
            image = operate(residual)
            new = dot(residual, residual)
            product = dot(residual, image)
            ratio = new / now
            alpha = new / (product - ratio * new / alpha)
            direction = add(residual, direction, ratio)
            along = add(image, along, ratio)
            now = new
    return surface


def kernel(
    nby, nbx, nlev,
    sideh, verth, thickh, t1h, t2h, uh, vh, levh, cdh, dgh,
    o1h, o2h, surf,
    side, vert, thick, t, u, v, levi, o, row_up, row_dn, got_dn, got_up, col_rt, col_lf, got_lf, got_rt,
    lv, fall_in, fld, h_up, h_dn, h_rt, h_lf, h_cn, v1r, v2r, mom, gath,
    load_sem, out_sem, send_a, recv_a, send_b, recv_b, send_c, recv_c, gsend, grecv,
):
    by, bx = lax.axis_index("by"), lax.axis_index("bx")
    total = nby * nbx
    me = by * nbx + bx
    ny, nx = fld.shape[1], fld.shape[2]

    loads = [
        pltpu.make_async_copy(sideh, side, load_sem.at[7]),
        pltpu.make_async_copy(verth, vert, load_sem.at[8]),
        pltpu.make_async_copy(thickh, thick, load_sem.at[9]),
        pltpu.make_async_copy(levh, levi, load_sem.at[4]),
        pltpu.make_async_copy(t1h, t.at[0], load_sem.at[0]),
        pltpu.make_async_copy(t2h, t.at[1], load_sem.at[1]),
        pltpu.make_async_copy(uh, u, load_sem.at[2]),
        pltpu.make_async_copy(vh, v, load_sem.at[3]),
        pltpu.make_async_copy(cdh, fld.at[1], load_sem.at[5]),
        pltpu.make_async_copy(dgh, fld.at[2], load_sem.at[6]),
    ]
    for copy in loads:
        copy.start()

    def neighbour(dy, dx):
        y, x = by + dy % nby, bx + dx % nbx
        return (jnp.where(y >= nby, y - nby, y), jnp.where(x >= nbx, x - nbx, x))

    others = [(dy, dx) for dy in range(nby) for dx in range(nbx)][1:]
    barrier = pltpu.get_barrier_semaphore()
    for dy, dx in others:
        pl.semaphore_signal(barrier, inc=1, device_id=neighbour(dy, dx), device_id_type=MESH)

    up_ok = jnp.where(by < nby - 1, 1.0, 0.0).astype(f32)
    dn_ok = jnp.where(by > 0, 1.0, 0.0).astype(f32)

    for copy in loads[:4]:
        copy.wait()
    levels = levi[...]
    levf = levels.astype(f32)

    lane = lax.broadcasted_iota(jnp.int32, (ny, LANES), 1)
    row_up[pl.ds(72, 8), :] = jnp.broadcast_to(levf[ny - 1 : ny], (8, nx))
    row_dn[pl.ds(72, 8), :] = jnp.broadcast_to(levf[0:1], (8, nx))
    right = jnp.where(lane == 96, pltpu.roll(levf[:, nx - LANES :], 97, 1), 0.0)
    left = jnp.where(lane == 96, pltpu.roll(levf[:, :LANES], 96, 1), 0.0)
    for c in range(2):
        loads[4 + c].wait()
        for k in range(nlev):
            row_up[24 * c + k : 24 * c + k + 1, :] = t[c, k, ny - 1 : ny, :]
            row_dn[24 * c + k : 24 * c + k + 1, :] = t[c, k, 0:1, :]
            place = 32 * c + k
            right = jnp.where(lane == place, pltpu.roll(t[c, k, :, nx - LANES :], place + 1, 1), right)
            tile = t[c, k, :, :LANES]
            left = jnp.where(lane == place, pltpu.roll(tile, place, 1) if place else tile, left)
    loads[6].wait()
    for k in range(nlev):
        right = jnp.where(lane == 64 + k, pltpu.roll(u[k, :, nx - LANES :].astype(f32), 65 + k, 1), right)
    loads[7].wait()
    for k in range(nlev):
        row_up[48 + k : 49 + k, :] = v[k, ny - 16 :, :].astype(f32)[15:16]
    col_rt[...] = right
    col_lf[...] = left

    pl.semaphore_wait(barrier, total - 1)

    def send(src, dst, ssem, rsem, to):
        copy = pltpu.make_async_remote_copy(
            src_ref=src, dst_ref=dst, send_sem=ssem, recv_sem=rsem, device_id=to, device_id_type=MESH
        )
        copy.start()
        return copy

    edge = [
        send(row_up, got_dn, send_a.at[0], recv_a.at[0], neighbour(1, 0)),
        send(row_dn, got_up, send_a.at[1], recv_a.at[1], neighbour(-1, 0)),
        send(col_rt, got_lf, send_a.at[2], recv_a.at[2], neighbour(0, 1)),
        send(col_lf, got_rt, send_a.at[3], recv_a.at[3], neighbour(0, -1)),
    ]

    def rim(which, ssem, rsem):
        copies = []
        for n, (dy, dx) in enumerate(SIDES):
            rows = pl.ds(0, ny) if dy == 0 else (pl.ds(ny - 8, 8) if dy > 0 else pl.ds(0, 8))
            cols = pl.ds(0, nx) if dx == 0 else (pl.ds(nx - LANES, LANES) if dx > 0 else pl.ds(0, LANES))
            place = {0: h_dn, 1: h_up, 2: h_lf, 3: h_rt}.get(n)
            dst = h_cn.at[n - 4, which] if place is None else place.at[which]
            copies.append(send(fld.at[which, rows, cols], dst, ssem.at[n], rsem.at[n], neighbour(dy, dx)))
        return copies

    for copy in loads[8:]:
        copy.wait()
    fld[1] = fld[1] * jnp.where(levels > 0, 0.5, 0.0).astype(f32)
    fld[2] = fld[2] - SHIFT
    rim_fixed = rim(pl.ds(1, 2), send_b, recv_b)

    sub_c = lax.broadcasted_iota(jnp.int32, (CHUNK, nx), 0)
    lane_c = lax.broadcasted_iota(jnp.int32, (CHUNK, nx), 1)
    for r in range(0, ny, CHUNK):
        rows = slice(r, r + CHUNK)
        lev = levf[rows]
        lev_rt = jnp.where(lane_c == nx - 1, 0.0, pltpu.roll(lev, nx - 1, 1))
        above = levf[r + CHUNK : r + CHUNK + 1] if r + CHUNK < ny else 0.0
        lev_up = jnp.where(sub_c == CHUNK - 1, above, pltpu.roll(lev, CHUNK - 1, 0))
        lv[0, rows, :] = lev
        lv[1, rows, :] = jnp.minimum(lev, lev_rt)
        lv[2, rows, :] = jnp.minimum(lev, lev_up)
    fall_in[...] = jnp.zeros_like(fall_in)
    fld[0] = jnp.zeros((ny, nx), f32)

    def level(k, _):
        kf = k.astype(f32)
        s, vk, tk = side[k], vert[k], thick[k]
        below = jnp.minimum(k + 1, nlev - 1)
        last = [0.0, 0.0]
        for r in range(0, ny, CHUNK):
            rows = slice(r, r + CHUNK)
            lev = lv[0, rows, :]
            hu = 0.5 * u[k, rows, :].astype(f32)
            hv = 0.5 * v[k, rows, :].astype(f32)
            in_e, in_n = kf < lv[1, rows, :], kf < lv[2, rows, :]
            pe, qe = jnp.where(in_e, hu + s, 0.0), jnp.where(in_e, hu - s, 0.0)
            pn, qn = jnp.where(in_n, hv + s, 0.0), jnp.where(in_n, hv - s, 0.0)
            wet = kf < lev
            fall_w = jnp.where(kf + 1.0 < lev, vk, 0.0)
            news = []
            for c in range(2):
                here = t[c, k, rows, :]
                upper = pltpu.roll(here, CHUNK - 1, 0)
                if r + CHUNK < ny:
                    upper = jnp.where(sub_c == CHUNK - 1, t[c, k, r + CHUNK : r + CHUNK + 1, :], upper)
                east = pe * here + qe * pltpu.roll(here, nx - 1, 1)
                north = pn * here + qn * upper
                south = jnp.where(sub_c == 0, last[c], pltpu.roll(north, 1, 0))
                last[c] = north[CHUNK - 1 :]
                fall = fall_w * (t[c, below, rows, :] - here)
                new = here + (pltpu.roll(east, 1, 1) - east) + (south - north) + (fall - fall_in[c, rows, :])
                new = jnp.where(wet, new, 0.0)
                fall_in[c, rows, :] = fall
                o[c, k, rows, :] = new
                news.append(new)
            fld[0, rows, :] += tk * (news[0] - 0.5 * news[1])
        return 0

    lax.fori_loop(0, nlev, level, 0, unroll=UNROLL)

    k_sub = lax.broadcasted_iota(jnp.int32, (24, nx), 0)
    k_lane = lax.rem(lane, 32)
    side_sub = jnp.zeros((24, nx), f32)
    thick_sub = jnp.zeros((24, nx), f32)
    side_lane = jnp.zeros((8, LANES), f32)
    thick_lane = jnp.zeros((8, LANES), f32)
    for k in range(nlev):
        side_sub = jnp.where(k_sub == k, side[k], side_sub)
        thick_sub = jnp.where(k_sub == k, thick[k], thick_sub)
        side_lane = jnp.where(k_lane[:8] == k, side[k], side_lane)
        thick_lane = jnp.where(lane[:8] == k, thick[k], thick_lane)
        thick_lane = jnp.where(lane[:8] == 32 + k, -0.5 * thick[k], thick_lane)
    side_lane, thick_lane = (jnp.concatenate([x] * (ny // 8), axis=0) for x in (side_lane, thick_lane))

    for copy in edge:
        copy.wait_recv()

    def row_flux(lower, upper, ok):
        lowest = jnp.minimum(lower[72:73, :], upper[72:73, :]) * ok
        is_open = k_sub.astype(f32) < lowest
        half = 0.5 * lower[48:72, :]
        p, q = jnp.where(is_open, half + side_sub, 0.0), jnp.where(is_open, half - side_sub, 0.0)
        out = []
        for c in range(2):
            flux = p * lower[24 * c : 24 * c + 24, :] + q * upper[24 * c : 24 * c + 24, :]
            out.append(jnp.where(is_open, flux, 0.0))
        return out

    def col_flux(came, beyond):
        half = 0.5 * jnp.where(lane < 32, pltpu.roll(came, 64, 1), pltpu.roll(came, 96, 1))
        lowest = jnp.minimum(came[:, 96:97], beyond[:, 96:97])
        flux = (half + side_lane) * came + (half - side_lane) * beyond
        return jnp.where(k_lane.astype(f32) < lowest, flux, 0.0)

    flux_dn = row_flux(got_dn, row_dn, dn_ok)
    flux_up = row_flux(row_up, got_up, up_ok)
    flux_lf = col_flux(got_lf[...], col_lf[...])
    flux_rt = col_flux(col_rt[...], got_rt[...])

    def weighed(flux):
        return jnp.sum(thick_sub * (flux[0] - 0.5 * flux[1]), axis=0, keepdims=True)

    fld[0, 0:1, :] += weighed(flux_dn)
    fld[0, ny - 1 : ny, :] -= weighed(flux_up)
    fld[0, :, :LANES] += jnp.where(lane == 0, jnp.sum(thick_lane * flux_lf, axis=1, keepdims=True), 0.0)
    fld[0, :, nx - LANES :] -= jnp.where(lane == LANES - 1, jnp.sum(thick_lane * flux_rt, axis=1, keepdims=True), 0.0)
    rim_force = rim(0, send_c, recv_c)

    outs = []
    for c, dst in enumerate((o1h, o2h)):
        for k in range(nlev):
            o[c, k, 0:1, :] += flux_dn[c][k : k + 1]
            o[c, k, ny - 1 : ny, :] -= flux_up[c][k : k + 1]
            place = 32 * c + k
            o[c, k, :, :LANES] += jnp.where(lane == 0, pltpu.roll(flux_lf, LANES - place, 1) if place else flux_lf, 0.0)
            o[c, k, :, nx - LANES :] -= jnp.where(lane == LANES - 1, pltpu.roll(flux_rt, LANES - 1 - place, 1), 0.0)
        outs.append(pltpu.make_async_copy(o.at[c], dst, out_sem.at[c]))
        outs[c].start()

    sub8 = lax.broadcasted_iota(jnp.int32, (8, nx), 0) < 4
    sub8c = sub8[:, :LANES]
    lane8 = lax.broadcasted_iota(jnp.int32, (8, LANES), 1) < 64
    lane64 = lane < 64
    row = lax.broadcasted_iota(jnp.int32, (ny + 8, nx + LANES), 0)
    mask = jnp.where(row < ny, 1.0, jnp.where(row < ny + 4, up_ok, dn_ok)).astype(f32)

    def widened(n):
        beside = jnp.where(lane64, h_rt[n], h_lf[n])
        ends = jnp.where(sub8, h_up[n], h_dn[n])
        corner = jnp.where(
            sub8c, jnp.where(lane8, h_cn[3, n], h_cn[2, n]), jnp.where(lane8, h_cn[1, n], h_cn[0, n])
        )
        top = jnp.concatenate([fld[n], beside], axis=1)
        bottom = jnp.concatenate([ends, corner], axis=1)
        return jnp.concatenate([top, bottom], axis=0) * mask

    for copy in rim_fixed:
        copy.wait_recv()
    depth, diag = widened(1), widened(2)
    for copy in rim_force:
        copy.wait_recv()
    tall, wide = ny + 8, nx + LANES

    def operate(a):
        b = pltpu.roll(a, wide - 1, 1)
        cc = pltpu.roll(a, tall - 1, 0)
        d = pltpu.roll(b, tall - 1, 0)
        p = depth * (d - a)
        q = depth * (b - cc)
        return (diag * a - p + pltpu.roll(q, 1, 1) + pltpu.roll(pltpu.roll(p, 1, 1) - q, 1, 0)) * mask

    def moment(a, b):
        prod = a[:ny, :nx] * b[:ny, :nx]
        prod = jnp.sum(prod.reshape(ny // 8, 8, nx), axis=0)
        prod = sum(prod[:, n : n + LANES] for n in range(0, nx, LANES))
        return jnp.sum(prod, axis=0, keepdims=True)

    w0 = widened(0)
    w1 = operate(w0)
    w2 = operate(w1)
    w3 = operate(w2)
    v1r[...] = w1[:ny, :nx]
    v2r[...] = w2[:ny, :nx]
    pairs = ((w0, w0), (w0, w1), (w1, w1), (w1, w2), (w2, w2), (w2, w3))
    mom[...] = jnp.concatenate([moment(a, b) for a, b in pairs] + [jnp.zeros((2, LANES), f32)], axis=0)

    for dy, dx in others:
        send(mom, gath.at[me], gsend, grecv, neighbour(dy, dx))
    gath[me] = mom[...]
    for copy in edge + rim_fixed + rim_force:
        copy.wait_send()
    for copy in outs:
        copy.wait()
    every = gath.at[pl.ds(0, total - 1)]
    pltpu.make_async_copy(every, every, grecv).wait()
    sums = jnp.sum(jnp.sum(gath[...], axis=0), axis=1, keepdims=True)
    moments = [jnp.broadcast_to(sums[n : n + 1], (8, LANES)) for n in range(6)]
    weights = [jnp.concatenate([x] * (nx // LANES), axis=1) for x in iterate_weights(moments)]
    for r in range(0, ny, 8):
        rows = slice(r, r + 8)
        surf[rows, :] = weights[0] * fld[0, rows, :] + weights[1] * v1r[rows, :] + weights[2] * v2r[rows, :]
    pltpu.make_async_copy(every, every, gsend).wait()


def on_device(nby, nbx, t1, t2, u, v, lev, side, vert, thick, cd, dg):
    nlev, ny, nx = t1.shape
    anywhere = pl.BlockSpec(memory_space=pl.ANY)
    vmem = pltpu.VMEM
    dma = pltpu.SemaphoreType.DMA
    cells = nlev * ny * nx
    return pl.pallas_call(
        functools.partial(kernel, nby, nbx, nlev),
        out_shape=(
            jax.ShapeDtypeStruct(t1.shape, f32),
            jax.ShapeDtypeStruct(t1.shape, f32),
            jax.ShapeDtypeStruct((ny, nx), f32),
        ),
        in_specs=[anywhere] * 10,
        out_specs=(anywhere, anywhere, pl.BlockSpec(memory_space=vmem)),
        scratch_shapes=[pltpu.SMEM((nlev,), f32)] * 3
        + [
            vmem((2, nlev, ny, nx), f32),
            vmem((nlev, ny, nx), u.dtype),
            vmem((nlev, ny, nx), v.dtype),
            vmem((ny, nx), jnp.int32),
            vmem((2, nlev, ny, nx), f32),
            vmem((80, nx), f32),
            vmem((80, nx), f32),
            vmem((80, nx), f32),
            vmem((80, nx), f32),
            vmem((ny, LANES), f32),
            vmem((ny, LANES), f32),
            vmem((ny, LANES), f32),
            vmem((ny, LANES), f32),
            vmem((3, ny, nx), f32),
            vmem((2, ny, nx), f32),
            vmem((3, ny, nx), f32),
            vmem((3, 8, nx), f32),
            vmem((3, 8, nx), f32),
            vmem((3, ny, LANES), f32),
            vmem((3, ny, LANES), f32),
            vmem((4, 3, 8, LANES), f32),
            vmem((ny, nx), f32),
            vmem((ny, nx), f32),
            vmem((8, LANES), f32),
            vmem((nby * nbx, 8, LANES), f32),
            dma((10,)),
            dma((2,)),
            dma((4,)),
            dma((4,)),
            dma((8,)),
            dma((8,)),
            dma((8,)),
            dma((8,)),
            dma,
            dma,
        ],
        compiler_params=pltpu.CompilerParams(
            collective_id=0, has_side_effects=True, vmem_limit_bytes=VMEM_MIB * 2**20
        ),
        cost_estimate=pl.CostEstimate(flops=60 * cells, bytes_accessed=20 * cells, transcendentals=0),
    )(side, vert, thick, t1, t2, u, v, lev, cd, dg)


def solution(mesh):
    def body(t1, t2, u, v, lev, side, vert, thick, cd, dg):
        return on_device(mesh.shape["by"], mesh.shape["bx"], t1, t2, u, v, lev, side, vert, thick, cd, dg)

    block, plane = P(None, "by", "bx"), P("by", "bx")
    return jax.shard_map(
        body,
        mesh=mesh,
        in_specs=(block, block, block, block, plane, P(), P(), P(), plane, plane),
        out_specs=(block, block, plane),
        check_vma=False,
    )
```

time: 49.7 us -> 28.1 us (0.57)
  Pallas kernels: 36.8 us -> 23.2 us
  local copies, waits for them, and re-layouts: 11.8 us -> 4.13 us
    pallas_call x1, Pallas kernels: 36.8 us -> 23.2 us  [on_device(): pl.pallas_call(functools.partial(kernel, nby, nbx, nlev), out_shape=(jax....]
    unnamed x23 -> x7, local copies, waits for them, and re-layouts: 11.8 us -> 4.13 us
where the time goes in v2:
time: 28.1 us; the launch traced here: 28 us
  Pallas kernels  23.2 us (83%)
  local copies, waits for them, and re-layouts  4.13 us (15%)
  between operations  0.65 us (2%)
    pallas_call x1, Pallas kernels, on_device(): pl.pallas_call(functools.partial(kernel, nby, nbx, nlev), out_shape=(jax....  23.2 us
    unnamed x7, local copies, waits for them, and re-layouts  4.13 us

profile of v2, /device:TPU:0, one launch (start us, length us, event | category | flops | bytes accessed | tf_op | source)
XLA Modules:
  0.0 28.0 jit_solution(5304086404436693890)
XLA Ops:
  0.6 23.2 %shard_map.121 = (f32[18,64,256]{2,1,0:T(8,128)}, f32[18,64,256]{2,1,0:T(8,128)}, f32[64,256]{1,0:T(8,128)}) custom-call(f32[18]{0:T(128)} %sideh.1, f32[18]{0:T(128)} %verth.1, f32[18]{0:T(128)} %thickh.1, f32[18,64,256]{2,1,0:T(8,128)} %t1h.1, f32[18,64,256]{2,1,0:T(8,128)} %t2h.1, bf16[18,64,256]{2,1,0:T(8,128)(2,1)} %uh.1, bf16[18,64,256]{2,1,0:T(8,128)(2,1)} %vh.1, ...), custom_call_target="tpu_custom_call" | custom-call | flops 17694720 | bytes 5898240 | tf_op jit(solution)/shard_map/pallas_call | solution.py:349
  23.8 0.0 copy-start
  23.8 2.5 %copy.16 = f32[18,64,256]{2,1,0:T(8,128)} copy(f32[18,64,256]{2,1,0:T(8,128)} %get-tuple-element.6) | data formatting | bytes 2359296
  26.3 0.0 copy-done
  26.3 0.0 copy-start.1
  26.3 1.0 %copy.17 = f32[18,64,256]{2,1,0:T(8,128)} copy(f32[18,64,256]{2,1,0:T(8,128)S(1)} %copy-done) | data formatting | bytes 2359296
  27.3 0.0 copy-done.1
  27.3 0.6 %copy.18 = f32[64,256]{1,0:T(8,128)} copy(f32[64,256]{1,0:T(8,128)S(1)} %copy-done.1) | data formatting | bytes 131072
Async XLA Ops:
  23.8 2.5 %copy-start = (f32[18,64,256]{2,1,0:T(8,128)S(1)}, f32[18,64,256]{2,1,0:T(8,128)}, u32[]{:S(2)}) copy-start(f32[18,64,256]{2,1,0:T(8,128)} %get-tuple-element.7) | copy-start | bytes 3538948
  26.3 1.0 %copy-start.1 = (f32[64,256]{1,0:T(8,128)S(1)}, f32[64,256]{1,0:T(8,128)}, u32[]{:S(2)}) copy-start(f32[64,256]{1,0:T(8,128)} %get-tuple-element.8) | copy-start | bytes 196612

commit v3 on v2

--- a/solution.py
+++ b/solution.py
@@ -10,7 +10,10 @@
 ITERS = 3
 SHIFT = 3.0
 CHUNK = 16
+PARTS = 3
 UNROLL = 2
+EARLY = 6
+SPLIT = 8
 VMEM_MIB = 62
 LANES = 128
 MESH = pl.DeviceIdType.MESH
@@ -71,7 +74,7 @@
     sideh, verth, thickh, t1h, t2h, uh, vh, levh, cdh, dgh,
     o1h, o2h, surf,
     side, vert, thick, t, u, v, levi, o, row_up, row_dn, got_dn, got_up, col_rt, col_lf, got_lf, got_rt,
-    lv, fall_in, fld, h_up, h_dn, h_rt, h_lf, h_cn, v1r, v2r, mom, gath,
+    lv, sums, fall_in, fld, h_up, h_dn, h_rt, h_lf, h_cn, v1r, v2r, mom, gath,
     load_sem, out_sem, send_a, recv_a, send_b, recv_b, send_c, recv_c, gsend, grecv,
 ):
     by, bx = lax.axis_index("by"), lax.axis_index("bx")
@@ -80,18 +83,26 @@
     ny, nx = fld.shape[1], fld.shape[2]
 
     loads = [
-        pltpu.make_async_copy(sideh, side, load_sem.at[7]),
-        pltpu.make_async_copy(verth, vert, load_sem.at[8]),
-        pltpu.make_async_copy(thickh, thick, load_sem.at[9]),
-        pltpu.make_async_copy(levh, levi, load_sem.at[4]),
-        pltpu.make_async_copy(t1h, t.at[0], load_sem.at[0]),
-        pltpu.make_async_copy(t2h, t.at[1], load_sem.at[1]),
-        pltpu.make_async_copy(uh, u, load_sem.at[2]),
-        pltpu.make_async_copy(vh, v, load_sem.at[3]),
-        pltpu.make_async_copy(cdh, fld.at[1], load_sem.at[5]),
-        pltpu.make_async_copy(dgh, fld.at[2], load_sem.at[6]),
+        pltpu.make_async_copy(sideh, side, load_sem.at[8]),
+        pltpu.make_async_copy(verth, vert, load_sem.at[9]),
+        pltpu.make_async_copy(thickh, thick, load_sem.at[10]),
+        pltpu.make_async_copy(levh, levi, load_sem.at[11]),
     ]
-    for copy in loads:
+    groups = ((0, EARLY), (EARLY, nlev))
+    bulk = []
+    for g, (first, end) in enumerate(groups):
+        span = pl.ds(first, end - first)
+        bulk.append([
+            pltpu.make_async_copy(t1h.at[span], t.at[0, span], load_sem.at[4 * g]),
+            pltpu.make_async_copy(t2h.at[span], t.at[1, span], load_sem.at[4 * g + 1]),
+            pltpu.make_async_copy(uh.at[span], u.at[span], load_sem.at[4 * g + 2]),
+            pltpu.make_async_copy(vh.at[span], v.at[span], load_sem.at[4 * g + 3]),
+        ])
+    planes = [
+        pltpu.make_async_copy(cdh, fld.at[1], load_sem.at[12]),
+        pltpu.make_async_copy(dgh, fld.at[2], load_sem.at[13]),
+    ]
+    for copy in loads + bulk[0] + bulk[1] + planes:
         copy.start()
 
     def neighbour(dy, dx):
@@ -106,65 +117,10 @@
     up_ok = jnp.where(by < nby - 1, 1.0, 0.0).astype(f32)
     dn_ok = jnp.where(by > 0, 1.0, 0.0).astype(f32)
 
-    for copy in loads[:4]:
+    for copy in loads:
         copy.wait()
     levels = levi[...]
     levf = levels.astype(f32)
-
-    lane = lax.broadcasted_iota(jnp.int32, (ny, LANES), 1)
-    row_up[pl.ds(72, 8), :] = jnp.broadcast_to(levf[ny - 1 : ny], (8, nx))
-    row_dn[pl.ds(72, 8), :] = jnp.broadcast_to(levf[0:1], (8, nx))
-    right = jnp.where(lane == 96, pltpu.roll(levf[:, nx - LANES :], 97, 1), 0.0)
-    left = jnp.where(lane == 96, pltpu.roll(levf[:, :LANES], 96, 1), 0.0)
-    for c in range(2):
-        loads[4 + c].wait()
-        for k in range(nlev):
-            row_up[24 * c + k : 24 * c + k + 1, :] = t[c, k, ny - 1 : ny, :]
-            row_dn[24 * c + k : 24 * c + k + 1, :] = t[c, k, 0:1, :]
-            place = 32 * c + k
-            right = jnp.where(lane == place, pltpu.roll(t[c, k, :, nx - LANES :], place + 1, 1), right)
-            tile = t[c, k, :, :LANES]
-            left = jnp.where(lane == place, pltpu.roll(tile, place, 1) if place else tile, left)
-    loads[6].wait()
-    for k in range(nlev):
-        right = jnp.where(lane == 64 + k, pltpu.roll(u[k, :, nx - LANES :].astype(f32), 65 + k, 1), right)
-    loads[7].wait()
-    for k in range(nlev):
-        row_up[48 + k : 49 + k, :] = v[k, ny - 16 :, :].astype(f32)[15:16]
-    col_rt[...] = right
-    col_lf[...] = left
-
-    pl.semaphore_wait(barrier, total - 1)
-
-    def send(src, dst, ssem, rsem, to):
-        copy = pltpu.make_async_remote_copy(
-            src_ref=src, dst_ref=dst, send_sem=ssem, recv_sem=rsem, device_id=to, device_id_type=MESH
-        )
-        copy.start()
-        return copy
-
-    edge = [
-        send(row_up, got_dn, send_a.at[0], recv_a.at[0], neighbour(1, 0)),
-        send(row_dn, got_up, send_a.at[1], recv_a.at[1], neighbour(-1, 0)),
-        send(col_rt, got_lf, send_a.at[2], recv_a.at[2], neighbour(0, 1)),
-        send(col_lf, got_rt, send_a.at[3], recv_a.at[3], neighbour(0, -1)),
-    ]
-
-    def rim(which, ssem, rsem):
-        copies = []
-        for n, (dy, dx) in enumerate(SIDES):
-            rows = pl.ds(0, ny) if dy == 0 else (pl.ds(ny - 8, 8) if dy > 0 else pl.ds(0, 8))
-            cols = pl.ds(0, nx) if dx == 0 else (pl.ds(nx - LANES, LANES) if dx > 0 else pl.ds(0, LANES))
-            place = {0: h_dn, 1: h_up, 2: h_lf, 3: h_rt}.get(n)
-            dst = h_cn.at[n - 4, which] if place is None else place.at[which]
-            copies.append(send(fld.at[which, rows, cols], dst, ssem.at[n], rsem.at[n], neighbour(dy, dx)))
-        return copies
-
-    for copy in loads[8:]:
-        copy.wait()
-    fld[1] = fld[1] * jnp.where(levels > 0, 0.5, 0.0).astype(f32)
-    fld[2] = fld[2] - SHIFT
-    rim_fixed = rim(pl.ds(1, 2), send_b, recv_b)
 
     sub_c = lax.broadcasted_iota(jnp.int32, (CHUNK, nx), 0)
     lane_c = lax.broadcasted_iota(jnp.int32, (CHUNK, nx), 1)
@@ -177,12 +133,107 @@
         lv[0, rows, :] = lev
         lv[1, rows, :] = jnp.minimum(lev, lev_rt)
         lv[2, rows, :] = jnp.minimum(lev, lev_up)
-    fall_in[...] = jnp.zeros_like(fall_in)
-    fld[0] = jnp.zeros((ny, nx), f32)
+    def force_pass(g):
+        start, end = groups[g]
+
+        def rows_of(n, _):
+            r = pl.multiple_of(n * CHUNK, CHUNK)
+            rows = pl.ds(r, CHUNK)
+            above = jnp.minimum(r + CHUNK, ny - 1)
+            lev, lev_e, lev_n = lv[0, rows, :], lv[1, rows, :], lv[2, rows, :]
+            before = None
+            if start:
+                before = t[0, start - 1, rows, :] - 0.5 * t[1, start - 1, rows, :]
+                acc = [sums[m, rows, :] for m in range(3)]
+            else:
+                acc = [jnp.zeros((CHUNK, nx), f32)] * 3
+            for k in range(start, end):
+                g_here = t[0, k, rows, :] - 0.5 * t[1, k, rows, :]
+                top = t[0, k, pl.ds(above, 1), :] - 0.5 * t[1, k, pl.ds(above, 1), :]
+                g_up = jnp.where(sub_c == CHUNK - 1, top, pltpu.roll(g_here, CHUNK - 1, 0))
+                g_rt = pltpu.roll(g_here, nx - 1, 1)
+                twice = 2.0 * side[k]
+                east = u[k, rows, :].astype(f32) * (g_here + g_rt) - twice * (g_rt - g_here)
+                north = v[k, rows, :].astype(f32) * (g_here + g_up) - twice * (g_up - g_here)
+                inside = thick[k] * g_here
+                if k:
+                    inside = inside + (vert[k - 1] * (thick[k - 1] - thick[k])) * (g_here - before)
+                half = 0.5 * thick[k]
+                acc[0] = acc[0] + jnp.where(lev > k, inside, 0.0)
+                acc[1] = acc[1] + half * jnp.where(lev_e > k, east, 0.0)
+                acc[2] = acc[2] + half * jnp.where(lev_n > k, north, 0.0)
+                before = g_here
+            for m in range(3):
+                sums[m, rows, :] = acc[m]
+            return 0
+
+        lax.fori_loop(0, ny // CHUNK, rows_of, 0)
+
+    for copy in bulk[0]:
+        copy.wait()
+    force_pass(0)
+    for copy in bulk[1]:
+        copy.wait()
+
+    lane = lax.broadcasted_iota(jnp.int32, (ny, LANES), 1)
+    row_up[pl.ds(72, 8), :] = jnp.broadcast_to(levf[ny - 1 : ny], (8, nx))
+    row_dn[pl.ds(72, 8), :] = jnp.broadcast_to(levf[0:1], (8, nx))
+    right = jnp.where(lane == 96, pltpu.roll(levf[:, nx - LANES :], 97, 1), 0.0)
+    left = jnp.where(lane == 96, pltpu.roll(levf[:, :LANES], 96, 1), 0.0)
+    for c in range(2):
+        for k in range(nlev):
+            row_up[24 * c + k : 24 * c + k + 1, :] = t[c, k, ny - 1 : ny, :]
+            row_dn[24 * c + k : 24 * c + k + 1, :] = t[c, k, 0:1, :]
+            place = 32 * c + k
+            right = jnp.where(lane == place, pltpu.roll(t[c, k, :, nx - LANES :], place + 1, 1), right)
+            tile = t[c, k, :, :LANES]
+            left = jnp.where(lane == place, pltpu.roll(tile, place, 1) if place else tile, left)
+    for k in range(nlev):
+        right = jnp.where(lane == 64 + k, pltpu.roll(u[k, :, nx - LANES :].astype(f32), 65 + k, 1), right)
+    for k in range(nlev):
+        row_up[48 + k : 49 + k, :] = v[k, ny - 16 :, :].astype(f32)[15:16]
+    col_rt[...] = right
+    col_lf[...] = left
+
+    pl.semaphore_wait(barrier, total - 1)
+
+    def send(src, dst, ssem, rsem, to):
+        copy = pltpu.make_async_remote_copy(
+            src_ref=src, dst_ref=dst, send_sem=ssem, recv_sem=rsem, device_id=to, device_id_type=MESH
+        )
+        copy.start()
+        return copy
+
+    edge = [
+        send(row_up, got_dn, send_a.at[0], recv_a.at[0], neighbour(1, 0)),
+        send(row_dn, got_up, send_a.at[1], recv_a.at[1], neighbour(-1, 0)),
+        send(col_rt, got_lf, send_a.at[2], recv_a.at[2], neighbour(0, 1)),
+        send(col_lf, got_rt, send_a.at[3], recv_a.at[3], neighbour(0, -1)),
+    ]
+
+    def rim(which, ssem, rsem):
+        copies = []
+        for n, (dy, dx) in enumerate(SIDES):
+            rows = pl.ds(0, ny) if dy == 0 else (pl.ds(ny - 8, 8) if dy > 0 else pl.ds(0, 8))
+            cols = pl.ds(0, nx) if dx == 0 else (pl.ds(nx - LANES, LANES) if dx > 0 else pl.ds(0, LANES))
+            place = {0: h_dn, 1: h_up, 2: h_lf, 3: h_rt}.get(n)
+            dst = h_cn.at[n - 4, which] if place is None else place.at[which]
+            copies.append(send(fld.at[which, rows, cols], dst, ssem.at[n], rsem.at[n], neighbour(dy, dx)))
+        return copies
+
+    for copy in planes:
+        copy.wait()
+    fld[1] = fld[1] * jnp.where(levels > 0, 0.5, 0.0).astype(f32)
+    fld[2] = fld[2] - SHIFT
+    rim_fixed = rim(pl.ds(1, 2), send_b, recv_b)
+
+    force_pass(1)
+    force = sums[0] + (pltpu.roll(sums[1], 1, 1) - sums[1]) + (pltpu.roll(sums[2], 1, 0) - sums[2])
+    fld[0] = force
 
     def level(k, _):
         kf = k.astype(f32)
-        s, vk, tk = side[k], vert[k], thick[k]
+        s, vk = side[k], vert[k]
         below = jnp.minimum(k + 1, nlev - 1)
         last = [0.0, 0.0]
         for r in range(0, ny, CHUNK):
@@ -195,7 +246,6 @@
             pn, qn = jnp.where(in_n, hv + s, 0.0), jnp.where(in_n, hv - s, 0.0)
             wet = kf < lev
             fall_w = jnp.where(kf + 1.0 < lev, vk, 0.0)
-            news = []
             for c in range(2):
                 here = t[c, k, rows, :]
                 upper = pltpu.roll(here, CHUNK - 1, 0)
@@ -210,11 +260,7 @@
                 new = jnp.where(wet, new, 0.0)
                 fall_in[c, rows, :] = fall
                 o[c, k, rows, :] = new
-                news.append(new)
-            fld[0, rows, :] += tk * (news[0] - 0.5 * news[1])
         return 0
-
-    lax.fori_loop(0, nlev, level, 0, unroll=UNROLL)
 
     k_sub = lax.broadcasted_iota(jnp.int32, (24, nx), 0)
     k_lane = lax.rem(lane, 32)
@@ -265,15 +311,23 @@
     rim_force = rim(0, send_c, recv_c)
 
     outs = []
-    for c, dst in enumerate((o1h, o2h)):
-        for k in range(nlev):
-            o[c, k, 0:1, :] += flux_dn[c][k : k + 1]
-            o[c, k, ny - 1 : ny, :] -= flux_up[c][k : k + 1]
-            place = 32 * c + k
-            o[c, k, :, :LANES] += jnp.where(lane == 0, pltpu.roll(flux_lf, LANES - place, 1) if place else flux_lf, 0.0)
-            o[c, k, :, nx - LANES :] -= jnp.where(lane == LANES - 1, pltpu.roll(flux_rt, LANES - 1 - place, 1), 0.0)
-        outs.append(pltpu.make_async_copy(o.at[c], dst, out_sem.at[c]))
-        outs[c].start()
+
+    def tracer_pass(first, end):
+        lax.fori_loop(first, end, level, 0, unroll=UNROLL)
+        for c, dst in enumerate((o1h, o2h)):
+            for k in range(first, end):
+                o[c, k, 0:1, :] += flux_dn[c][k : k + 1]
+                o[c, k, ny - 1 : ny, :] -= flux_up[c][k : k + 1]
+                place = 32 * c + k
+                o[c, k, :, :LANES] += jnp.where(lane == 0, pltpu.roll(flux_lf, LANES - place, 1) if place else flux_lf, 0.0)
+                o[c, k, :, nx - LANES :] -= jnp.where(lane == LANES - 1, pltpu.roll(flux_rt, LANES - 1 - place, 1), 0.0)
+            span = pl.ds(first, end - first)
+            copy = pltpu.make_async_copy(o.at[c, span], dst.at[span], out_sem.at[len(outs)])
+            copy.start()
+            outs.append(copy)
+
+    fall_in[...] = jnp.zeros_like(fall_in)
+    tracer_pass(0, SPLIT)
 
     sub8 = lax.broadcasted_iota(jnp.int32, (8, nx), 0) < 4
     sub8c = sub8[:, :LANES]
@@ -325,14 +379,15 @@
     for dy, dx in others:
         send(mom, gath.at[me], gsend, grecv, neighbour(dy, dx))
     gath[me] = mom[...]
+    tracer_pass(SPLIT, nlev)
     for copy in edge + rim_fixed + rim_force:
         copy.wait_send()
     for copy in outs:
         copy.wait()
     every = gath.at[pl.ds(0, total - 1)]
     pltpu.make_async_copy(every, every, grecv).wait()
-    sums = jnp.sum(jnp.sum(gath[...], axis=0), axis=1, keepdims=True)
-    moments = [jnp.broadcast_to(sums[n : n + 1], (8, LANES)) for n in range(6)]
+    whole = jnp.sum(jnp.sum(gath[...], axis=0), axis=1, keepdims=True)
+    moments = [jnp.broadcast_to(whole[n : n + 1], (8, LANES)) for n in range(6)]
     weights = [jnp.concatenate([x] * (nx // LANES), axis=1) for x in iterate_weights(moments)]
     for r in range(0, ny, 8):
         rows = slice(r, r + 8)
@@ -346,7 +401,7 @@
     vmem = pltpu.VMEM
     dma = pltpu.SemaphoreType.DMA
     cells = nlev * ny * nx
-    return pl.pallas_call(
+    made = pl.pallas_call(
         functools.partial(kernel, nby, nbx, nlev),
         out_shape=(
             jax.ShapeDtypeStruct(t1.shape, f32),
@@ -371,6 +426,7 @@
             vmem((ny, LANES), f32),
             vmem((ny, LANES), f32),
             vmem((3, ny, nx), f32),
+            vmem((3, ny, nx), f32),
             vmem((2, ny, nx), f32),
             vmem((3, ny, nx), f32),
             vmem((3, 8, nx), f32),
@@ -382,8 +438,8 @@
             vmem((ny, nx), f32),
             vmem((8, LANES), f32),
             vmem((nby * nbx, 8, LANES), f32),
-            dma((10,)),
-            dma((2,)),
+            dma((14,)),
+            dma((4,)),
             dma((4,)),
             dma((4,)),
             dma((8,)),
@@ -399,6 +455,29 @@
         cost_estimate=pl.CostEstimate(flops=60 * cells, bytes_accessed=20 * cells, transcendentals=0),
     )(side, vert, thick, t1, t2, u, v, lev, cd, dg)
 
+    return pl.pallas_call(
+        hand_on,
+        out_shape=tuple(jax.ShapeDtypeStruct(x.shape, x.dtype) for x in made),
+        in_specs=[anywhere] * 3,
+        out_specs=(anywhere,) * 3,
+        scratch_shapes=[dma((2 * PARTS + 1,))],
+        compiler_params=pltpu.CompilerParams(vmem_limit_bytes=VMEM_MIB * 2**20),
+        cost_estimate=pl.CostEstimate(flops=0, bytes_accessed=16 * cells, transcendentals=0),
+    )(*made)
+
+
+def hand_on(a, b, c, a_out, b_out, c_out, sems):
+    copies = [pltpu.make_async_copy(c, c_out, sems.at[2 * PARTS])]
+    step = a.shape[0] // PARTS
+    for n in range(PARTS):
+        span = pl.ds(n * step, step)
+        copies.append(pltpu.make_async_copy(a.at[span], a_out.at[span], sems.at[2 * n]))
+        copies.append(pltpu.make_async_copy(b.at[span], b_out.at[span], sems.at[2 * n + 1]))
+    for copy in copies:
+        copy.start()
+    for copy in copies:
+        copy.wait()
+
 
 def solution(mesh):
     def body(t1, t2, u, v, lev, side, vert, thick, cd, dg):

time: 28.1 us -> 98.8 us (3.52)
  Pallas kernels: 23.2 us -> 98 us
  local copies, waits for them, and re-layouts: 4.13 us -> 0 us
    pallas_call x0 -> x1, Pallas kernels: none -> 74.6 us  [on_device(): pl.pallas_call(hand_on, out_shape=tuple((jax.ShapeDtypeStruct(x.shape, x....]
    unnamed x7 -> x0, local copies, waits for them, and re-layouts: 4.13 us -> none
where the time goes in v3:
time: 98.8 us; the launch traced here: 98.7 us
  Pallas kernels  98 us (99%)
    pallas_call x1, Pallas kernels, on_device(): pl.pallas_call(hand_on, out_shape=tuple((jax.ShapeDtypeStruct(x.shape, x....  74.6 us
    pallas_call x1, Pallas kernels, on_device(): pl.pallas_call(functools.partial(kernel, nby, nbx, nlev), out_shape=(jax....  23.4 us

profile of v3, /device:TPU:0, one launch (start us, length us, event | category | flops | bytes accessed | tf_op | source)
XLA Modules:
  0.0 98.7 jit_solution(11671041561541498604)
XLA Ops:
  0.6 23.4 %shard_map.121 = (f32[18,64,256]{2,1,0:T(8,128)}, f32[18,64,256]{2,1,0:T(8,128)}, f32[64,256]{1,0:T(8,128)}) custom-call(f32[18]{0:T(128)} %sideh.1, f32[18]{0:T(128)} %verth.1, f32[18]{0:T(128)} %thickh.1, f32[18,64,256]{2,1,0:T(8,128)} %t1h.1, f32[18,64,256]{2,1,0:T(8,128)} %t2h.1, bf16[18,64,256]{2,1,0:T(8,128)(2,1)} %uh.1, bf16[18,64,256]{2,1,0:T(8,128)(2,1)} %vh.1, ...), custom_call_target="tpu_custom_call" | custom-call | flops 17694720 | bytes 5898240 | tf_op jit(solution)/shard_map/pallas_call | solution.py:404
  24.1 74.6 %shard_map.122 = (f32[18,64,256]{2,1,0:T(8,128)}, f32[18,64,256]{2,1,0:T(8,128)}, f32[64,256]{1,0:T(8,128)}) custom-call(f32[18,64,256]{2,1,0:T(8,128)} %get-tuple-element.6.a, f32[18,64,256]{2,1,0:T(8,128)} %get-tuple-element.7.b, f32[64,256]{1,0:T(8,128)} %get-tuple-element.8.c), custom_call_target="tpu_custom_call" | custom-call | bytes 4718592 | tf_op jit(solution)/shard_map/pallas_call | solution.py:458

commit v4 on v3

--- a/solution.py
+++ b/solution.py
@@ -11,7 +11,6 @@
 SHIFT = 3.0
 CHUNK = 16
 PARTS = 3
-UNROLL = 2
 EARLY = 6
 SPLIT = 8
 VMEM_MIB = 62
@@ -74,7 +73,7 @@
     sideh, verth, thickh, t1h, t2h, uh, vh, levh, cdh, dgh,
     o1h, o2h, surf,
     side, vert, thick, t, u, v, levi, o, row_up, row_dn, got_dn, got_up, col_rt, col_lf, got_lf, got_rt,
-    lv, sums, fall_in, fld, h_up, h_dn, h_rt, h_lf, h_cn, v1r, v2r, mom, gath,
+    lv, sums, fall_in, flx, rows_up, cols, fld, h_up, h_dn, h_rt, h_lf, h_cn, v1r, v2r, mom, gath,
     load_sem, out_sem, send_a, recv_a, send_b, recv_b, send_c, recv_c, gsend, grecv,
 ):
     by, bx = lax.axis_index("by"), lax.axis_index("bx")
@@ -182,16 +181,21 @@
     left = jnp.where(lane == 96, pltpu.roll(levf[:, :LANES], 96, 1), 0.0)
     for c in range(2):
         for k in range(nlev):
-            row_up[24 * c + k : 24 * c + k + 1, :] = t[c, k, ny - 1 : ny, :]
-            row_dn[24 * c + k : 24 * c + k + 1, :] = t[c, k, 0:1, :]
             place = 32 * c + k
             right = jnp.where(lane == place, pltpu.roll(t[c, k, :, nx - LANES :], place + 1, 1), right)
             tile = t[c, k, :, :LANES]
             left = jnp.where(lane == place, pltpu.roll(tile, place, 1) if place else tile, left)
     for k in range(nlev):
         right = jnp.where(lane == 64 + k, pltpu.roll(u[k, :, nx - LANES :].astype(f32), 65 + k, 1), right)
+    for c in range(2):
+        upper = [t[c, k, ny - 1 : ny, :] for k in range(nlev)]
+        lower = [t[c, k, 0:1, :] for k in range(nlev)]
+        for k in range(nlev):
+            row_up[24 * c + k : 24 * c + k + 1, :] = upper[k]
+            row_dn[24 * c + k : 24 * c + k + 1, :] = lower[k]
+    upper = [v[k, ny - 16 :, :].astype(f32)[15:16] for k in range(nlev)]
     for k in range(nlev):
-        row_up[48 + k : 49 + k, :] = v[k, ny - 16 :, :].astype(f32)[15:16]
+        row_up[48 + k : 49 + k, :] = upper[k]
     col_rt[...] = right
     col_lf[...] = left
 
@@ -230,37 +234,6 @@
     force_pass(1)
     force = sums[0] + (pltpu.roll(sums[1], 1, 1) - sums[1]) + (pltpu.roll(sums[2], 1, 0) - sums[2])
     fld[0] = force
-
-    def level(k, _):
-        kf = k.astype(f32)
-        s, vk = side[k], vert[k]
-        below = jnp.minimum(k + 1, nlev - 1)
-        last = [0.0, 0.0]
-        for r in range(0, ny, CHUNK):
-            rows = slice(r, r + CHUNK)
-            lev = lv[0, rows, :]
-            hu = 0.5 * u[k, rows, :].astype(f32)
-            hv = 0.5 * v[k, rows, :].astype(f32)
-            in_e, in_n = kf < lv[1, rows, :], kf < lv[2, rows, :]
-            pe, qe = jnp.where(in_e, hu + s, 0.0), jnp.where(in_e, hu - s, 0.0)
-            pn, qn = jnp.where(in_n, hv + s, 0.0), jnp.where(in_n, hv - s, 0.0)
-            wet = kf < lev
-            fall_w = jnp.where(kf + 1.0 < lev, vk, 0.0)
-            for c in range(2):
-                here = t[c, k, rows, :]
-                upper = pltpu.roll(here, CHUNK - 1, 0)
-                if r + CHUNK < ny:
-                    upper = jnp.where(sub_c == CHUNK - 1, t[c, k, r + CHUNK : r + CHUNK + 1, :], upper)
-                east = pe * here + qe * pltpu.roll(here, nx - 1, 1)
-                north = pn * here + qn * upper
-                south = jnp.where(sub_c == 0, last[c], pltpu.roll(north, 1, 0))
-                last[c] = north[CHUNK - 1 :]
-                fall = fall_w * (t[c, below, rows, :] - here)
-                new = here + (pltpu.roll(east, 1, 1) - east) + (south - north) + (fall - fall_in[c, rows, :])
-                new = jnp.where(wet, new, 0.0)
-                fall_in[c, rows, :] = fall
-                o[c, k, rows, :] = new
-        return 0
 
     k_sub = lax.broadcasted_iota(jnp.int32, (24, nx), 0)
     k_lane = lax.rem(lane, 32)
@@ -311,22 +284,77 @@
     rim_force = rim(0, send_c, recv_c)
 
     outs = []
+    for c in range(2):
+        flx[c] = flux_dn[c]
+        rows_up[c] = flux_up[c]
+    cols[0] = flux_lf
+    cols[1] = flux_rt
+    fall_in[...] = jnp.zeros_like(fall_in)
+    lane_t = lane[:CHUNK]
 
     def tracer_pass(first, end):
-        lax.fori_loop(first, end, level, 0, unroll=UNROLL)
+        def rows_of(n, _):
+            r = pl.multiple_of(n * CHUNK, CHUNK)
+            rows = pl.ds(r, CHUNK)
+            above = jnp.minimum(r + CHUNK, ny - 1)
+            lev, lev_e, lev_n = lv[0, rows, :], lv[1, rows, :], lv[2, rows, :]
+            from_lf, from_rt = cols[0, rows, :], cols[1, rows, :]
+            falls = [fall_in[c, rows, :] for c in range(2)]
+            pending = []
+            for k in range(first, end):
+                here = [t[c, k, rows, :] for c in range(2)]
+                top = [t[c, k, pl.ds(above, 1), :] for c in range(2)]
+                under = [flx[c, k : k + 1, :] for c in range(2)]
+                below = [t[c, k + 1, rows, :] for c in range(2)] if k + 1 < nlev else None
+                hu = 0.5 * u[k, rows, :].astype(f32)
+                hv = 0.5 * v[k, rows, :].astype(f32)
+                for ref, where, value in pending:
+                    ref[where] = value
+                pending = []
+                s = side[k]
+                in_e, in_n = lev_e > k, lev_n > k
+                pe, qe = jnp.where(in_e, hu + s, 0.0), jnp.where(in_e, hu - s, 0.0)
+                pn, qn = jnp.where(in_n, hv + s, 0.0), jnp.where(in_n, hv - s, 0.0)
+                wet = lev > k
+                if k + 1 < nlev:
+                    fall_w = jnp.where(lev > k + 1, vert[k], 0.0)
+                for c in range(2):
+                    x = here[c]
+                    up = jnp.where(sub_c == CHUNK - 1, top[c], pltpu.roll(x, CHUNK - 1, 0))
+                    east = pe * x + qe * pltpu.roll(x, nx - 1, 1)
+                    north = pn * x + qn * up
+                    south = jnp.where(sub_c == 0, under[c], pltpu.roll(north, 1, 0))
+                    place = 32 * c + k
+                    lf = pltpu.roll(from_lf, LANES - place, 1) if place else from_lf
+                    rt = pltpu.roll(from_rt, LANES - 1 - place, 1)
+                    shared = jnp.concatenate(
+                        [jnp.where(lane_t == 0, lf, 0.0)]
+                        + [jnp.zeros((CHUNK, LANES), f32)] * (nx // LANES - 2)
+                        + [jnp.where(lane_t == LANES - 1, -rt, 0.0)],
+                        axis=1,
+                    )
+                    new = x + (pltpu.roll(east, 1, 1) - east + shared) + (south - north) - falls[c]
+                    if k + 1 < nlev:
+                        falls[c] = fall_w * (below[c] - x)
+                        new = new + falls[c]
+                    pending.append((o, (c, k, rows), jnp.where(wet, new, 0.0)))
+                    pending.append((flx, (c, slice(k, k + 1)), north[CHUNK - 1 :]))
+            for ref, where, value in pending:
+                ref[where] = value
+            for c in range(2):
+                fall_in[c, rows, :] = falls[c]
+            return 0
+
+        lax.fori_loop(0, ny // CHUNK, rows_of, 0)
+        span = pl.ds(first, end - first)
         for c, dst in enumerate((o1h, o2h)):
+            ends = [o[c, k, ny - 1 : ny, :] - rows_up[c, k : k + 1, :] for k in range(first, end)]
             for k in range(first, end):
-                o[c, k, 0:1, :] += flux_dn[c][k : k + 1]
-                o[c, k, ny - 1 : ny, :] -= flux_up[c][k : k + 1]
-                place = 32 * c + k
-                o[c, k, :, :LANES] += jnp.where(lane == 0, pltpu.roll(flux_lf, LANES - place, 1) if place else flux_lf, 0.0)
-                o[c, k, :, nx - LANES :] -= jnp.where(lane == LANES - 1, pltpu.roll(flux_rt, LANES - 1 - place, 1), 0.0)
-            span = pl.ds(first, end - first)
+                o[c, k, ny - 1 : ny, :] = ends[k - first]
             copy = pltpu.make_async_copy(o.at[c, span], dst.at[span], out_sem.at[len(outs)])
             copy.start()
             outs.append(copy)
 
-    fall_in[...] = jnp.zeros_like(fall_in)
     tracer_pass(0, SPLIT)
 
     sub8 = lax.broadcasted_iota(jnp.int32, (8, nx), 0) < 4
@@ -428,6 +456,9 @@
             vmem((3, ny, nx), f32),
             vmem((3, ny, nx), f32),
             vmem((2, ny, nx), f32),
+            vmem((2, 24, nx), f32),
+            vmem((2, 24, nx), f32),
+            vmem((2, ny, LANES), f32),
             vmem((3, ny, nx), f32),
             vmem((3, 8, nx), f32),
             vmem((3, 8, nx), f32),
@@ -460,22 +491,27 @@
         out_shape=tuple(jax.ShapeDtypeStruct(x.shape, x.dtype) for x in made),
         in_specs=[anywhere] * 3,
         out_specs=(anywhere,) * 3,
-        scratch_shapes=[dma((2 * PARTS + 1,))],
+        scratch_shapes=[vmem((2, nlev, ny, nx), f32), vmem((ny, nx), f32), dma((2, 2 * PARTS + 1))],
         compiler_params=pltpu.CompilerParams(vmem_limit_bytes=VMEM_MIB * 2**20),
         cost_estimate=pl.CostEstimate(flops=0, bytes_accessed=16 * cells, transcendentals=0),
     )(*made)
 
 
-def hand_on(a, b, c, a_out, b_out, c_out, sems):
-    copies = [pltpu.make_async_copy(c, c_out, sems.at[2 * PARTS])]
+def hand_on(a, b, c, a_out, b_out, c_out, stage, plane, sems):
     step = a.shape[0] // PARTS
+    moves = [(c, plane, c_out)]
     for n in range(PARTS):
         span = pl.ds(n * step, step)
-        copies.append(pltpu.make_async_copy(a.at[span], a_out.at[span], sems.at[2 * n]))
-        copies.append(pltpu.make_async_copy(b.at[span], b_out.at[span], sems.at[2 * n + 1]))
-    for copy in copies:
+        moves.append((a.at[span], stage.at[0, span], a_out.at[span]))
+        moves.append((b.at[span], stage.at[1, span], b_out.at[span]))
+    ins = [pltpu.make_async_copy(src, via, sems.at[0, n]) for n, (src, via, _) in enumerate(moves)]
+    outs = [pltpu.make_async_copy(via, dst, sems.at[1, n]) for n, (_, via, dst) in enumerate(moves)]
+    for copy in ins:
         copy.start()
-    for copy in copies:
+    for come, go in zip(ins, outs):
+        come.wait()
+        go.start()
+    for copy in outs:
         copy.wait()
 
 

time: 98.8 us -> 26.8 us (0.27)
  Pallas kernels: 98 us -> 26 us
    pallas_call x1, Pallas kernels: 74.6 us -> 2.55 us  [on_device(): pl.pallas_call(hand_on, out_shape=tuple((jax.ShapeDtypeStruct(x.shape, x....]
where the time goes in v4:
time: 26.8 us; the launch traced here: 26.6 us
  Pallas kernels  26 us (97%)
  between operations  0.64 us (2%)
    pallas_call x1, Pallas kernels, on_device(): pl.pallas_call(functools.partial(kernel, nby, nbx, nlev), out_shape=(jax....  23.4 us
    pallas_call x1, Pallas kernels, on_device(): pl.pallas_call(hand_on, out_shape=tuple((jax.ShapeDtypeStruct(x.shape, x....  2.55 us

profile of v4, /device:TPU:0, one launch (start us, length us, event | category | flops | bytes accessed | tf_op | source)
XLA Modules:
  0.0 26.6 jit_solution(15711542372288037870)
XLA Ops:
  0.6 23.4 %shard_map.121 = (f32[18,64,256]{2,1,0:T(8,128)}, f32[18,64,256]{2,1,0:T(8,128)}, f32[64,256]{1,0:T(8,128)}) custom-call(f32[18]{0:T(128)} %sideh.1, f32[18]{0:T(128)} %verth.1, f32[18]{0:T(128)} %thickh.1, f32[18,64,256]{2,1,0:T(8,128)} %t1h.1, f32[18,64,256]{2,1,0:T(8,128)} %t2h.1, bf16[18,64,256]{2,1,0:T(8,128)(2,1)} %uh.1, bf16[18,64,256]{2,1,0:T(8,128)(2,1)} %vh.1, ...), custom_call_target="tpu_custom_call" | custom-call | flops 17694720 | bytes 5898240 | tf_op jit(solution)/shard_map/pallas_call | solution.py:432
  24.1 2.5 %shard_map.122 = (f32[18,64,256]{2,1,0:T(8,128)}, f32[18,64,256]{2,1,0:T(8,128)}, f32[64,256]{1,0:T(8,128)}) custom-call(f32[18,64,256]{2,1,0:T(8,128)} %get-tuple-element.6.a, f32[18,64,256]{2,1,0:T(8,128)} %get-tuple-element.7.b, f32[64,256]{1,0:T(8,128)} %get-tuple-element.8.c), custom_call_target="tpu_custom_call" | custom-call | bytes 4718592 | tf_op jit(solution)/shard_map/pallas_call | solution.py:489

commit v5 on v4

--- a/solution.py
+++ b/solution.py
@@ -10,6 +10,7 @@
 ITERS = 3
 SHIFT = 3.0
 CHUNK = 16
+WIDE = 16
 PARTS = 3
 EARLY = 6
 SPLIT = 8
@@ -73,13 +74,22 @@
     sideh, verth, thickh, t1h, t2h, uh, vh, levh, cdh, dgh,
     o1h, o2h, surf,
     side, vert, thick, t, u, v, levi, o, row_up, row_dn, got_dn, got_up, col_rt, col_lf, got_lf, got_rt,
-    lv, sums, fall_in, flx, rows_up, cols, fld, h_up, h_dn, h_rt, h_lf, h_cn, v1r, v2r, mom, gath,
+    lv, sums, fall_in, flx, rows_up, cols, fld, h_up, h_dn, h_rt, h_lf, narrow, h_cn, v1r, v2r, mom, gath,
     load_sem, out_sem, send_a, recv_a, send_b, recv_b, send_c, recv_c, gsend, grecv,
 ):
     by, bx = lax.axis_index("by"), lax.axis_index("bx")
     total = nby * nbx
     me = by * nbx + bx
     ny, nx = fld.shape[1], fld.shape[2]
+
+    def neighbour(dy, dx):
+        y, x = by + dy % nby, bx + dx % nbx
+        return (jnp.where(y >= nby, y - nby, y), jnp.where(x >= nbx, x - nbx, x))
+
+    others = [(dy, dx) for dy in range(nby) for dx in range(nbx)][1:]
+    barrier = pltpu.get_barrier_semaphore()
+    for dy, dx in others:
+        pl.semaphore_signal(barrier, inc=1, device_id=neighbour(dy, dx), device_id_type=MESH)
 
     loads = [
         pltpu.make_async_copy(sideh, side, load_sem.at[8]),
@@ -103,15 +113,6 @@
     ]
     for copy in loads + bulk[0] + bulk[1] + planes:
         copy.start()
-
-    def neighbour(dy, dx):
-        y, x = by + dy % nby, bx + dx % nbx
-        return (jnp.where(y >= nby, y - nby, y), jnp.where(x >= nbx, x - nbx, x))
-
-    others = [(dy, dx) for dy in range(nby) for dx in range(nbx)][1:]
-    barrier = pltpu.get_barrier_semaphore()
-    for dy, dx in others:
-        pl.semaphore_signal(barrier, inc=1, device_id=neighbour(dy, dx), device_id_type=MESH)
 
     up_ok = jnp.where(by < nby - 1, 1.0, 0.0).astype(f32)
     dn_ok = jnp.where(by > 0, 1.0, 0.0).astype(f32)
@@ -175,8 +176,8 @@
         copy.wait()
 
     lane = lax.broadcasted_iota(jnp.int32, (ny, LANES), 1)
-    row_up[pl.ds(72, 8), :] = jnp.broadcast_to(levf[ny - 1 : ny], (8, nx))
-    row_dn[pl.ds(72, 8), :] = jnp.broadcast_to(levf[0:1], (8, nx))
+    row_up[pl.ds(48, 8), :] = jnp.broadcast_to(levf[ny - 1 : ny], (8, nx))
+    row_dn[pl.ds(48, 8), :] = jnp.broadcast_to(levf[0:1], (8, nx))
     right = jnp.where(lane == 96, pltpu.roll(levf[:, nx - LANES :], 97, 1), 0.0)
     left = jnp.where(lane == 96, pltpu.roll(levf[:, :LANES], 96, 1), 0.0)
     for c in range(2):
@@ -195,7 +196,7 @@
             row_dn[24 * c + k : 24 * c + k + 1, :] = lower[k]
     upper = [v[k, ny - 16 :, :].astype(f32)[15:16] for k in range(nlev)]
     for k in range(nlev):
-        row_up[48 + k : 49 + k, :] = upper[k]
+        row_up[56 + k : 57 + k, :] = upper[k]
     col_rt[...] = right
     col_lf[...] = left
 
@@ -215,20 +216,36 @@
         send(col_lf, got_rt, send_a.at[3], recv_a.at[3], neighbour(0, -1)),
     ]
 
+    lane_8 = lane[:8]
+
+    def fold(n):
+        right = left = jnp.zeros((8, LANES), f32)
+        for g in range(ny // 8):
+            rows = slice(8 * g, 8 * g + 8)
+            mine = (lane_8 >= WIDE * g) & (lane_8 < WIDE * g + WIDE)
+            right = jnp.where(mine, pltpu.roll(fld[n, rows, nx - LANES :], (WIDE * g + WIDE) % LANES, 1), right)
+            tile = fld[n, rows, :LANES]
+            left = jnp.where(mine, pltpu.roll(tile, WIDE * g, 1) if g else tile, left)
+        narrow[0, n] = right
+        narrow[1, n] = left
+
     def rim(which, ssem, rsem):
         copies = []
         for n, (dy, dx) in enumerate(SIDES):
-            rows = pl.ds(0, ny) if dy == 0 else (pl.ds(ny - 8, 8) if dy > 0 else pl.ds(0, 8))
+            rows = pl.ds(ny - 8, 8) if dy > 0 else pl.ds(0, 8)
             cols = pl.ds(0, nx) if dx == 0 else (pl.ds(nx - LANES, LANES) if dx > 0 else pl.ds(0, LANES))
             place = {0: h_dn, 1: h_up, 2: h_lf, 3: h_rt}.get(n)
             dst = h_cn.at[n - 4, which] if place is None else place.at[which]
-            copies.append(send(fld.at[which, rows, cols], dst, ssem.at[n], rsem.at[n], neighbour(dy, dx)))
+            src = fld.at[which, rows, cols] if dy else narrow.at[n - 2, which]
+            copies.append(send(src, dst, ssem.at[n], rsem.at[n], neighbour(dy, dx)))
         return copies
 
     for copy in planes:
         copy.wait()
     fld[1] = fld[1] * jnp.where(levels > 0, 0.5, 0.0).astype(f32)
     fld[2] = fld[2] - SHIFT
+    fold(1)
+    fold(2)
     rim_fixed = rim(pl.ds(1, 2), send_b, recv_b)
 
     force_pass(1)
@@ -253,9 +270,9 @@
         copy.wait_recv()
 
     def row_flux(lower, upper, ok):
-        lowest = jnp.minimum(lower[72:73, :], upper[72:73, :]) * ok
+        lowest = jnp.minimum(lower[48:49, :], upper[48:49, :]) * ok
         is_open = k_sub.astype(f32) < lowest
-        half = 0.5 * lower[48:72, :]
+        half = 0.5 * lower[56:80, :]
         p, q = jnp.where(is_open, half + side_sub, 0.0), jnp.where(is_open, half - side_sub, 0.0)
         out = []
         for c in range(2):
@@ -281,6 +298,7 @@
     fld[0, ny - 1 : ny, :] -= weighed(flux_up)
     fld[0, :, :LANES] += jnp.where(lane == 0, jnp.sum(thick_lane * flux_lf, axis=1, keepdims=True), 0.0)
     fld[0, :, nx - LANES :] -= jnp.where(lane == LANES - 1, jnp.sum(thick_lane * flux_rt, axis=1, keepdims=True), 0.0)
+    fold(0)
     rim_force = rim(0, send_c, recv_c)
 
     outs = []
@@ -360,12 +378,17 @@
     sub8 = lax.broadcasted_iota(jnp.int32, (8, nx), 0) < 4
     sub8c = sub8[:, :LANES]
     lane8 = lax.broadcasted_iota(jnp.int32, (8, LANES), 1) < 64
-    lane64 = lane < 64
     row = lax.broadcasted_iota(jnp.int32, (ny + 8, nx + LANES), 0)
     mask = jnp.where(row < ny, 1.0, jnp.where(row < ny + 4, up_ok, dn_ok)).astype(f32)
 
     def widened(n):
-        beside = jnp.where(lane64, h_rt[n], h_lf[n])
+        pieces = []
+        for g in range(ny // 8):
+            right = pltpu.roll(h_rt[n], LANES - WIDE * g, 1) if g else h_rt[n]
+            shift = (LANES - WIDE - WIDE * g) % LANES
+            left = pltpu.roll(h_lf[n], shift, 1) if shift else h_lf[n]
+            pieces.append(jnp.where(lane8, right, left))
+        beside = jnp.concatenate(pieces, axis=0)
         ends = jnp.where(sub8, h_up[n], h_dn[n])
         corner = jnp.where(
             sub8c, jnp.where(lane8, h_cn[3, n], h_cn[2, n]), jnp.where(lane8, h_cn[1, n], h_cn[0, n])
@@ -446,9 +469,9 @@
             vmem((ny, nx), jnp.int32),
             vmem((2, nlev, ny, nx), f32),
             vmem((80, nx), f32),
+            vmem((56, nx), f32),
             vmem((80, nx), f32),
-            vmem((80, nx), f32),
-            vmem((80, nx), f32),
+            vmem((56, nx), f32),
             vmem((ny, LANES), f32),
             vmem((ny, LANES), f32),
             vmem((ny, LANES), f32),
@@ -462,8 +485,9 @@
             vmem((3, ny, nx), f32),
             vmem((3, 8, nx), f32),
             vmem((3, 8, nx), f32),
-            vmem((3, ny, LANES), f32),
-            vmem((3, ny, LANES), f32),
+            vmem((3, 8, LANES), f32),
+            vmem((3, 8, LANES), f32),
+            vmem((2, 3, 8, LANES), f32),
             vmem((4, 3, 8, LANES), f32),
             vmem((ny, nx), f32),
             vmem((ny, nx), f32),

time: 26.8 us -> 26.5 us (0.989)
  Pallas kernels: 26 us -> 25.7 us
    pallas_call x1, Pallas kernels: 23.4 us -> 23.2 us  [on_device(): pl.pallas_call(functools.partial(kernel, nby, nbx, nlev), out_shape=(jax....]
where the time goes in v5:
time: 26.5 us; the launch traced here: 26.4 us
  Pallas kernels  25.7 us (97%)
  between operations  0.64 us (2%)
    pallas_call x1, Pallas kernels, on_device(): pl.pallas_call(functools.partial(kernel, nby, nbx, nlev), out_shape=(jax....  23.2 us
    pallas_call x1, Pallas kernels, on_device(): pl.pallas_call(hand_on, out_shape=tuple((jax.ShapeDtypeStruct(x.shape, x....  2.55 us

profile of v5, /device:TPU:0, one launch (start us, length us, event | category | flops | bytes accessed | tf_op | source)
XLA Modules:
  0.0 26.4 jit_solution(17821397539746756773)
XLA Ops:
  0.6 23.2 %shard_map.121 = (f32[18,64,256]{2,1,0:T(8,128)}, f32[18,64,256]{2,1,0:T(8,128)}, f32[64,256]{1,0:T(8,128)}) custom-call(f32[18]{0:T(128)} %sideh.1, f32[18]{0:T(128)} %verth.1, f32[18]{0:T(128)} %thickh.1, f32[18,64,256]{2,1,0:T(8,128)} %t1h.1, f32[18,64,256]{2,1,0:T(8,128)} %t2h.1, bf16[18,64,256]{2,1,0:T(8,128)(2,1)} %uh.1, bf16[18,64,256]{2,1,0:T(8,128)(2,1)} %vh.1, ...), custom_call_target="tpu_custom_call" | custom-call | flops 17694720 | bytes 5898240 | tf_op jit(solution)/shard_map/pallas_call | solution.py:455
  23.8 2.5 %shard_map.122 = (f32[18,64,256]{2,1,0:T(8,128)}, f32[18,64,256]{2,1,0:T(8,128)}, f32[64,256]{1,0:T(8,128)}) custom-call(f32[18,64,256]{2,1,0:T(8,128)} %get-tuple-element.6.a, f32[18,64,256]{2,1,0:T(8,128)} %get-tuple-element.7.b, f32[64,256]{1,0:T(8,128)} %get-tuple-element.8.c), custom_call_target="tpu_custom_call" | custom-call | bytes 4718592 | tf_op jit(solution)/shard_map/pallas_call | solution.py:513

commit v6 on v5

--- a/solution.py
+++ b/solution.py
@@ -11,9 +11,10 @@
 SHIFT = 3.0
 CHUNK = 16
 WIDE = 16
-PARTS = 3
+PARTS = 6
 EARLY = 6
 SPLIT = 8
+SECOND = 11
 VMEM_MIB = 62
 LANES = 128
 MESH = pl.DeviceIdType.MESH
@@ -74,21 +75,21 @@
     sideh, verth, thickh, t1h, t2h, uh, vh, levh, cdh, dgh,
     o1h, o2h, surf,
     side, vert, thick, t, u, v, levi, o, row_up, row_dn, got_dn, got_up, col_rt, col_lf, got_lf, got_rt,
-    lv, sums, fall_in, flx, rows_up, cols, fld, h_up, h_dn, h_rt, h_lf, narrow, h_cn, v1r, v2r, mom, gath,
+    lv, sums, fall_in, flx, rows_up, cols, fld, h_up, h_dn, h_rt, h_lf, narrow, h_cn, v1r, v2r, mom, part, gath_by, gath,
     load_sem, out_sem, send_a, recv_a, send_b, recv_b, send_c, recv_c, gsend, grecv,
 ):
     by, bx = lax.axis_index("by"), lax.axis_index("bx")
-    total = nby * nbx
-    me = by * nbx + bx
     ny, nx = fld.shape[1], fld.shape[2]
 
     def neighbour(dy, dx):
         y, x = by + dy % nby, bx + dx % nbx
         return (jnp.where(y >= nby, y - nby, y), jnp.where(x >= nbx, x - nbx, x))
 
-    others = [(dy, dx) for dy in range(nby) for dx in range(nbx)][1:]
+    column = [(dy, 0) for dy in range(1, nby)]
+    line = [(0, dx) for dx in range(1, nbx)]
+    partners = column + line + [(dy, dx) for dy, dx in SIDES if dy and dx]
     barrier = pltpu.get_barrier_semaphore()
-    for dy, dx in others:
+    for dy, dx in partners:
         pl.semaphore_signal(barrier, inc=1, device_id=neighbour(dy, dx), device_id_type=MESH)
 
     loads = [
@@ -169,10 +170,7 @@
 
         lax.fori_loop(0, ny // CHUNK, rows_of, 0)
 
-    for copy in bulk[0]:
-        copy.wait()
-    force_pass(0)
-    for copy in bulk[1]:
+    for copy in bulk[0] + bulk[1]:
         copy.wait()
 
     lane = lax.broadcasted_iota(jnp.int32, (ny, LANES), 1)
@@ -200,7 +198,7 @@
     col_rt[...] = right
     col_lf[...] = left
 
-    pl.semaphore_wait(barrier, total - 1)
+    pl.semaphore_wait(barrier, len(partners))
 
     def send(src, dst, ssem, rsem, to):
         copy = pltpu.make_async_remote_copy(
@@ -248,6 +246,7 @@
     fold(2)
     rim_fixed = rim(pl.ds(1, 2), send_b, recv_b)
 
+    force_pass(0)
     force_pass(1)
     force = sums[0] + (pltpu.roll(sums[1], 1, 1) - sums[1]) + (pltpu.roll(sums[2], 1, 0) - sums[2])
     fld[0] = force
@@ -427,23 +426,31 @@
     pairs = ((w0, w0), (w0, w1), (w1, w1), (w1, w2), (w2, w2), (w2, w3))
     mom[...] = jnp.concatenate([moment(a, b) for a, b in pairs] + [jnp.zeros((2, LANES), f32)], axis=0)
 
-    for dy, dx in others:
-        send(mom, gath.at[me], gsend, grecv, neighbour(dy, dx))
-    gath[me] = mom[...]
-    tracer_pass(SPLIT, nlev)
+    for dy, dx in column:
+        send(mom, gath_by.at[by], gsend.at[0], grecv.at[0], neighbour(dy, dx))
+    gath_by[by] = mom[...]
+    tracer_pass(SPLIT, SECOND)
+    rest = gath_by.at[pl.ds(0, nby - 1)]
+    pltpu.make_async_copy(rest, rest, grecv.at[0]).wait()
+    part[...] = jnp.sum(gath_by[...], axis=0)
+    for dy, dx in line:
+        send(part, gath.at[bx], gsend.at[1], grecv.at[1], neighbour(dy, dx))
+    gath[bx] = part[...]
+    tracer_pass(SECOND, nlev)
     for copy in edge + rim_fixed + rim_force:
         copy.wait_send()
-    for copy in outs:
-        copy.wait()
-    every = gath.at[pl.ds(0, total - 1)]
-    pltpu.make_async_copy(every, every, grecv).wait()
+    every = gath.at[pl.ds(0, nbx - 1)]
+    pltpu.make_async_copy(every, every, grecv.at[1]).wait()
     whole = jnp.sum(jnp.sum(gath[...], axis=0), axis=1, keepdims=True)
     moments = [jnp.broadcast_to(whole[n : n + 1], (8, LANES)) for n in range(6)]
     weights = [jnp.concatenate([x] * (nx // LANES), axis=1) for x in iterate_weights(moments)]
     for r in range(0, ny, 8):
         rows = slice(r, r + 8)
         surf[rows, :] = weights[0] * fld[0, rows, :] + weights[1] * v1r[rows, :] + weights[2] * v2r[rows, :]
-    pltpu.make_async_copy(every, every, gsend).wait()
+    pltpu.make_async_copy(rest, rest, gsend.at[0]).wait()
+    pltpu.make_async_copy(every, every, gsend.at[1]).wait()
+    for copy in outs:
+        copy.wait()
 
 
 def on_device(nby, nbx, t1, t2, u, v, lev, side, vert, thick, cd, dg):
@@ -492,17 +499,19 @@
             vmem((ny, nx), f32),
             vmem((ny, nx), f32),
             vmem((8, LANES), f32),
-            vmem((nby * nbx, 8, LANES), f32),
+            vmem((8, LANES), f32),
+            vmem((nby, 8, LANES), f32),
+            vmem((nbx, 8, LANES), f32),
             dma((14,)),
-            dma((4,)),
+            dma((6,)),
             dma((4,)),
             dma((4,)),
             dma((8,)),
             dma((8,)),
             dma((8,)),
             dma((8,)),
-            dma,
-            dma,
+            dma((2,)),
+            dma((2,)),
         ],
         compiler_params=pltpu.CompilerParams(
             collective_id=0, has_side_effects=True, vmem_limit_bytes=VMEM_MIB * 2**20

time: 26.5 us -> 27.6 us (1.042)
  Pallas kernels: 25.7 us -> 26.8 us
    pallas_call x1, Pallas kernels: 23.2 us -> 24.1 us  [on_device(): pl.pallas_call(functools.partial(kernel, nby, nbx, nlev), out_shape=(jax....]
where the time goes in v6:
time: 27.6 us; the launch traced here: 27.5 us
  Pallas kernels  26.8 us (97%)
  between operations  0.64 us (2%)
    pallas_call x1, Pallas kernels, on_device(): pl.pallas_call(functools.partial(kernel, nby, nbx, nlev), out_shape=(jax....  24.1 us
    pallas_call x1, Pallas kernels, on_device(): pl.pallas_call(hand_on, out_shape=tuple((jax.ShapeDtypeStruct(x.shape, x....  2.67 us

profile of v6, /device:TPU:0, one launch (start us, length us, event | category | flops | bytes accessed | tf_op | source)
XLA Modules:
  0.0 27.5 jit_solution(4708002771902635650)
XLA Ops:
  0.6 24.1 %shard_map.121 = (f32[18,64,256]{2,1,0:T(8,128)}, f32[18,64,256]{2,1,0:T(8,128)}, f32[64,256]{1,0:T(8,128)}) custom-call(f32[18]{0:T(128)} %sideh.1, f32[18]{0:T(128)} %verth.1, f32[18]{0:T(128)} %thickh.1, f32[18,64,256]{2,1,0:T(8,128)} %t1h.1, f32[18,64,256]{2,1,0:T(8,128)} %t2h.1, bf16[18,64,256]{2,1,0:T(8,128)(2,1)} %uh.1, bf16[18,64,256]{2,1,0:T(8,128)(2,1)} %vh.1, ...), custom_call_target="tpu_custom_call" | custom-call | flops 17694720 | bytes 5898240 | tf_op jit(solution)/shard_map/pallas_call | solution.py:462
  24.8 2.7 %shard_map.122 = (f32[18,64,256]{2,1,0:T(8,128)}, f32[18,64,256]{2,1,0:T(8,128)}, f32[64,256]{1,0:T(8,128)}) custom-call(f32[18,64,256]{2,1,0:T(8,128)} %get-tuple-element.6.a, f32[18,64,256]{2,1,0:T(8,128)} %get-tuple-element.7.b, f32[64,256]{1,0:T(8,128)} %get-tuple-element.8.c), custom_call_target="tpu_custom_call" | custom-call | bytes 4718592 | tf_op jit(solution)/shard_map/pallas_call | solution.py:522

commit v7 on v5

--- a/solution.py
+++ b/solution.py
@@ -169,10 +169,7 @@
 
         lax.fori_loop(0, ny // CHUNK, rows_of, 0)
 
-    for copy in bulk[0]:
-        copy.wait()
-    force_pass(0)
-    for copy in bulk[1]:
+    for copy in bulk[0] + bulk[1]:
         copy.wait()
 
     lane = lax.broadcasted_iota(jnp.int32, (ny, LANES), 1)
@@ -248,6 +245,7 @@
     fold(2)
     rim_fixed = rim(pl.ds(1, 2), send_b, recv_b)
 
+    force_pass(0)
     force_pass(1)
     force = sums[0] + (pltpu.roll(sums[1], 1, 1) - sums[1]) + (pltpu.roll(sums[2], 1, 0) - sums[2])
     fld[0] = force

time: 26.5 us -> 26.5 us (level)
  no operation moved by 1% of the time
where the time goes in v7:
time: 26.5 us; the launch traced here: 26.4 us
  Pallas kernels  25.7 us (97%)
  between operations  0.64 us (2%)
    pallas_call x1, Pallas kernels, on_device(): pl.pallas_call(functools.partial(kernel, nby, nbx, nlev), out_shape=(jax....  23.2 us
    pallas_call x1, Pallas kernels, on_device(): pl.pallas_call(hand_on, out_shape=tuple((jax.ShapeDtypeStruct(x.shape, x....  2.55 us

profile of v7, /device:TPU:0, one launch (start us, length us, event | category | flops | bytes accessed | tf_op | source)
XLA Modules:
  0.0 26.4 jit_solution(9130912891174102219)
XLA Ops:
  0.6 23.2 %shard_map.121 = (f32[18,64,256]{2,1,0:T(8,128)}, f32[18,64,256]{2,1,0:T(8,128)}, f32[64,256]{1,0:T(8,128)}) custom-call(f32[18]{0:T(128)} %sideh.1, f32[18]{0:T(128)} %verth.1, f32[18]{0:T(128)} %thickh.1, f32[18,64,256]{2,1,0:T(8,128)} %t1h.1, f32[18,64,256]{2,1,0:T(8,128)} %t2h.1, bf16[18,64,256]{2,1,0:T(8,128)(2,1)} %uh.1, bf16[18,64,256]{2,1,0:T(8,128)(2,1)} %vh.1, ...), custom_call_target="tpu_custom_call" | custom-call | flops 17694720 | bytes 5898240 | tf_op jit(solution)/shard_map/pallas_call | solution.py:453
  23.8 2.5 %shard_map.122 = (f32[18,64,256]{2,1,0:T(8,128)}, f32[18,64,256]{2,1,0:T(8,128)}, f32[64,256]{1,0:T(8,128)}) custom-call(f32[18,64,256]{2,1,0:T(8,128)} %get-tuple-element.6.a, f32[18,64,256]{2,1,0:T(8,128)} %get-tuple-element.7.b, f32[64,256]{1,0:T(8,128)} %get-tuple-element.8.c), custom_call_target="tpu_custom_call" | custom-call | bytes 4718592 | tf_op jit(solution)/shard_map/pallas_call | solution.py:511
